TPU v7x, 512 devices: a whole 4x4x16 slice. The times are simulated.
512 devices in a mesh: row: 32 (over x, y, core), col: 16 (over z).
Axes of the slice: x: 4, y: 4, z: 16, core: 2. Of those that a mesh axis runs over, the one named last changes fastest.
Arguments:
- transition: bfloat16 [8192, 8192], P('row', 'col'), may hold values from 0.0099487305 to 1
- tile_live: int32 [64, 64], replicated, may hold values from 0 to 1, as said below
- prune_keep: int32 [8192, 8192], P('row', 'col'), may hold values from 0 to 1, as said below
Outputs:
- next_strips: float32 [16, 512, 8192], P('col', 'row')
Inputs may be any that keep to these rules, and one draw needn't show every extreme that they name: `tile_live`: each aligned block of 2 x 4 tiles (the tiles of one device) holds 1 to 4 live tiles, exactly 4 in some block; every diagonal tile is live. `prune_keep`: every diagonal entry is 1.
All inputs are finite; a program needn't handle non-finite values.
Results may differ from a plain program's by a relative error of at most 0.0003.
Values may be sent and summed in bfloat16 or wider, within the bound.
No kernel may reach another device: no remote copies, remote signals or barrier semaphores. Data moves between devices by JAX's collectives and lax.ppermute only.
A program may use at most 128 MiB of HBM per device.

v0:
```python
import jax
import jax.numpy as jnp
from jax import lax
from jax.sharding import PartitionSpec as P

TILE = 128


def shards(transition, tile_live, prune_keep):
    rows_here, cols_here = transition.shape
    row_tiles = rows_here // TILE
    col_tiles = cols_here // TILE
    row_place = lax.axis_index("row")
    col_place = lax.axis_index("col")
    flags = lax.dynamic_slice(
        tile_live, (row_place * row_tiles, col_place * col_tiles), (row_tiles, col_tiles)
    )
    cells = jnp.repeat(jnp.repeat(flags, TILE, axis=0), TILE, axis=1).astype(jnp.bfloat16)
    masked = transition * cells
    row_panel = lax.all_gather(masked, "col", axis=1, tiled=True)
    nodes = row_panel.shape[1]
    expanded = jnp.dot(
        row_panel,
        lax.all_gather(masked, "row", axis=0, tiled=True),
        preferred_element_type=jnp.float32,
    )
    kept = expanded * prune_keep.astype(jnp.float32)
    inflated = kept * kept
    strip_rows = lax.all_to_all(inflated.T, "row", split_axis=0, concat_axis=1, tiled=True)
    strip_rows = nodes * strip_rows / jnp.sum(strip_rows, axis=1, keepdims=True)
    return strip_rows[None]


def solution(mesh):
    placed = (P("row", "col"), P(), P("row", "col"))
    return jax.shard_map(
        shards, mesh=mesh, in_specs=placed, out_specs=P("col", "row", None), check_vma=False
    )
```

profile of v0, /device:TPU:1, one launch (start us, length us, event | category | flops | bytes accessed | tf_op | source)
XLA Modules:
  0.0 194.4 jit_solution(10189699451448045149)
XLA Ops:
  6.5 0.0 all-gather.3.cloned.1.call-start
  6.5 0.8 dynamic-slice_convert_fusion
  7.3 0.3 broadcast_in_dim.9
  7.7 1.7 bitcast_multiply_fusion
  9.3 0.0 all-gather.3.cloned.1.call-update
  9.4 0.0 all-gather.5.cloned.1.call-start
  9.4 0.7 all-gather.5.cloned.1.call-update
  10.1 74.7 %all-gather.3.cloned.1.call-done = bf16[256,8192]{1,0:T(8,128)(2,1)} async-done(((bf16[256,512]{1,0:T(8,128)(2,1)}), bf16[256,8192]{1,0:T(8,128)(2,1)}) %all-gather.3.cloned.1.call-update) | async-done | bytes 4194320 | tf_op jit(solution)/shard_map/all_gather | solution.py:20
  84.8 77.2 %all-gather.5.cloned.1.call-done = bf16[8192,512]{1,0:T(8,128)(2,1)} async-done(((bf16[256,512]{1,0:T(8,128)(2,1)}), bf16[8192,512]{1,0:T(8,128)(2,1)}) %all-gather.5.cloned.1.call-update) | async-done | bytes 8388624 | tf_op jit(solution)/shard_map/all_gather | solution.py:24
  162.0 6.9 %fusion.1 = f32[512,256]{0,1:T(8,128)S(1)} fusion(bf16[256,8192]{1,0:T(8,128)(2,1)} %all-gather.3.cloned.1.call-done, bf16[8192,512]{1,0:T(8,128)(2,1)} %all-gather.5.cloned.1.call-done, s32[256,512]{1,0:T(8,128)} %param.5), kind=kOutput, calls=%fused_computation.2 | convolution fusion | flops 2147876864 | bytes 13631488 | tf_op jit(solution)/shard_map/dot_general | solution.py:22
  168.9 0.2 copy.6
  169.1 16.9 %all_to_all.13 = f32[32,16,256]{2,1,0:T(8,128)S(1)} all-to-all(f32[32,16,256]{2,1,0:T(8,128)S(1)} %bitcast.11), channel_id=1, replica_groups=mesh['row'=32,'col'=16] {'row'}, dimensions={0} | all-to-all | bytes 1048576 | tf_op jit(solution)/shard_map/all_to_all | solution.py:29
  186.0 0.2 fusion.2
  186.2 0.3 copy.7
  186.5 0.1 mul.42
  186.6 0.9 broadcast_divide_fusion
  (1 shorter events, 0.0 us)
Async XLA Ops:
  6.5 78.2 %all-gather.3.cloned.1.call-start = ((), (), s32[]{:S(2)}) async-start(), calls=%async_computation.1 | async-start | bytes 4456448 | tf_op jit(solution)/shard_map/all_gather | solution.py:20
  9.4 152.6 %all-gather.5.cloned.1.call-start = ((), (), s32[]{:S(2)}) async-start(), calls=%async_computation.2 | async-start | bytes 8650752 | tf_op jit(solution)/shard_map/all_gather | solution.py:24
Sparse Core Ops, SparseCore 0:
  9.5 75.2 all-gather.2
  87.9 73.9 all-gather.4
where the time goes:
time: 195 us; the launch traced here: 194 us
  waiting for transfers between devices  153 us (78%)
  blocking collectives  16.9 us (9%)
  between operations  13.4 us (7%)
  matrix products  6.94 us (4%)
  other arithmetic  3.58 us (2%)
    all_gather x1, waiting for transfers between devices, shards(): lax.all_gather(masked, 'row', axis=0, tiled=True)  77.2 us
    all_gather x1, waiting for transfers between devices, shards(): row_panel = lax.all_gather(masked, 'col', axis=1, tiled=True)  74.7 us
    all_to_all x1, blocking collectives, shards(): lax.all_to_all(inflated.T, 'row', split_axis=0, concat_axis=1, tiled=True)  16.9 us
    dot_general x1, matrix products, shards(): jnp.dot(row_panel, lax.all_gather(masked, 'row', axis=0, tiled=True), pre...  6.94 us
  transfers between devices with their start and end apart: 2, of which 2 were waited for; matrix products, arithmetic and copies ran while one was open for 0% of the time, Pallas kernels for 0%

commit v1 on v0

v1 whole, which is shorter than its diff:
```python
import jax
import jax.numpy as jnp
from jax import lax
from jax.experimental import pallas as pl
from jax.experimental.pallas import tpu as pltpu
from jax.sharding import PartitionSpec as P

TILE = 128
LIVE = 4
UNIT = 16384.0
STEPS = 4


def spots(rows, cols):
    return [(a, b, slice(a * TILE, (a + 1) * TILE), slice(b * TILE, (b + 1) * TILE)) for a in range(rows) for b in range(cols)]


def pack_body(live, x_ref, out_ref):
    rows, cols = x_ref.shape[0] // TILE, x_ref.shape[1] // TILE
    top, left = lax.axis_index("row") * rows, lax.axis_index("col") * cols
    slot = jnp.int32(0)
    for a, b, across, down in spots(rows, cols):
        flag = live[top + a, left + b]

        @pl.when((flag > 0) & (slot < LIVE))
        def _(slot=slot, across=across, down=down):
            units = x_ref[across, down].astype(jnp.float32) * UNIT
            out_ref[slot] = units.astype(jnp.int32).astype(jnp.int16)

        slot = slot + flag


def pack(tile_live, transition):
    return pl.pallas_call(
        pack_body,
        out_shape=jax.ShapeDtypeStruct((LIVE, TILE, TILE), jnp.int16),
        in_specs=[pl.BlockSpec(memory_space=pltpu.SMEM), pl.BlockSpec(memory_space=pltpu.VMEM)],
        out_specs=pl.BlockSpec(memory_space=pltpu.VMEM),
        name="pack",
    )(tile_live, transition)


def unpack(live, top, left, rows, cols, slots_ref, group, dense_ref, base):
    slot = jnp.int32(0)
    for a, b, across, down in spots(rows, cols):
        flag = live[top + a, left + b]
        tile = slots_ref[group, jnp.minimum(slot, LIVE - 1)].astype(jnp.float32)
        tile = jnp.where(flag > 0, tile, 0.0).astype(jnp.bfloat16)
        dense_ref[base + a * TILE : base + (a + 1) * TILE, down] = tile
        slot = slot + flag


def product_body(rows, cols, live, a_ref, b_ref, keep_ref, out_ref, a_dense, b_dense, total):
    step = pl.program_id(0)
    per = a_ref.shape[0]
    each = b_ref.shape[0] // per
    top, left = lax.axis_index("row") * rows, lax.axis_index("col") * cols

    @pl.when(step == 0)
    def _():
        total[...] = jnp.zeros_like(total)

    for p in range(per):
        panel = step * per + p
        unpack(live, top, panel * cols, rows, cols, a_ref, p, a_dense.at[p % 2], 0)
        for e in range(each):
            unpack(live, (panel * each + e) * rows, left, rows, cols, b_ref, p * each + e, b_dense.at[p % 2], e * rows * TILE)
        total[...] += jnp.dot(a_dense[p % 2], b_dense[p % 2], preferred_element_type=jnp.float32)

    @pl.when(step == pl.num_programs(0) - 1)
    def _():
        kept = total[...] * (keep_ref[...].astype(jnp.float32) * (1.0 / (UNIT * UNIT)))
        inflated = (kept * kept).T
        out_ref[...] = inflated.reshape(out_ref.shape)


def product(tile_live, row_panel, col_panel, keep):
    n_row, n_col = col_panel.shape[0], row_panel.shape[0]
    height, width = keep.shape
    rows, cols = height // TILE, width // TILE
    per = n_col // STEPS
    each = width // height
    return pl.pallas_call(
        lambda *refs: product_body(rows, cols, *refs),
        out_shape=jax.ShapeDtypeStruct((n_row, width // n_row, height), jnp.float32),
        grid=(STEPS,),
        in_specs=[
            pl.BlockSpec(memory_space=pltpu.SMEM),
            pl.BlockSpec((per, LIVE, TILE, TILE), lambda s: (s, 0, 0, 0)),
            pl.BlockSpec((per * each, LIVE, TILE, TILE), lambda s: (s, 0, 0, 0)),
            pl.BlockSpec((height, width), lambda s: (0, 0)),
        ],
        out_specs=pl.BlockSpec((n_row, width // n_row, height), lambda s: (0, 0, 0)),
        scratch_shapes=[
            pltpu.VMEM((2, height, width), jnp.bfloat16),
            pltpu.VMEM((2, width, width), jnp.bfloat16),
            pltpu.VMEM((height, width), jnp.float32),
        ],
        compiler_params=pltpu.CompilerParams(dimension_semantics=("arbitrary",), vmem_limit_bytes=32 * 1024 * 1024),
        name="product",
    )(tile_live, row_panel, col_panel, keep)


def scale_body(x_ref, out_ref):
    parts, _, height = x_ref.shape
    nodes = parts * height
    entries = x_ref[...]
    column_total = jnp.sum(jnp.sum(entries, axis=0), axis=1, keepdims=True)
    factor = nodes / column_total
    for p in range(parts):
        out_ref[0, :, p * height : (p + 1) * height] = entries[p] * factor


def scale(entries):
    parts, strips, height = entries.shape
    return pl.pallas_call(
        scale_body,
        out_shape=jax.ShapeDtypeStruct((1, strips, parts * height), jnp.float32),
        in_specs=[pl.BlockSpec(memory_space=pltpu.VMEM)],
        out_specs=pl.BlockSpec(memory_space=pltpu.VMEM),
        name="scale",
    )(entries)


def shards(transition, tile_live, prune_keep):
    packed = pack(tile_live, transition)
    row_panel = lax.all_gather(packed, "col", axis=0)
    col_panel = lax.all_gather(packed, "row", axis=0)
    strips = product(tile_live, row_panel, col_panel, prune_keep)
    entries = lax.all_to_all(strips, "row", split_axis=0, concat_axis=0, tiled=True)
    return scale(entries)


def solution(mesh):
    placed = (P("row", "col"), P(), P("row", "col"))
    return jax.shard_map(
        shards, mesh=mesh, in_specs=placed, out_specs=P("col", "row", None), check_vma=False
    )
```

time: 195 us -> 108 us (0.55)
  waiting for transfers between devices: 153 us -> 0 us
  blocking collectives: 16.9 us -> 96.3 us
  between operations: 13.4 us -> 0.02 us
  Pallas kernels: 0 us -> 11.8 us
  matrix products: 6.94 us -> 0 us
  other arithmetic: 3.58 us -> 0 us
    all_gather x2 -> x0, waiting for transfers between devices: 152 us -> none  [the longest x1 77.2 us: shards(): lax.all_gather(masked, 'row', axis=0, tiled=True)]
    all_gather x0 -> x2, blocking collectives: none -> 79.7 us  [the longest x1 44.8 us: shards(): row_panel = lax.all_gather(packed, 'col', axis=0)]
    pallas_call x0 -> x3, Pallas kernels: none -> 11.8 us  [the longest x1 7.67 us: product(): pl.pallas_call(lambda *refs: product_body(rows, cols, *refs), out_shape=j...]
    dot_general x1 -> x0, matrix products: 6.94 us -> none  [shards(): jnp.dot(row_panel, lax.all_gather(masked, 'row', axis=0, tiled=True), pre...]
  transfers between devices with their start and end apart: 2 -> 0, of which waited for: 2 -> 0; matrix products, arithmetic and copies ran while one was open for 0% -> 0% of each run, Pallas kernels for 0% -> 0%
where the time goes in v1:
time: 108 us
  blocking collectives  96.3 us (89%)
  Pallas kernels  11.8 us (11%)
    all_gather x1, blocking collectives, shards(): row_panel = lax.all_gather(packed, 'col', axis=0)  44.8 us
    all_gather x1, blocking collectives, shards(): col_panel = lax.all_gather(packed, 'row', axis=0)  34.9 us
    all_to_all x1, blocking collectives, shards(): lax.all_to_all(strips, 'row', split_axis=0, concat_axis=0, tiled=True)  16.6 us
    pallas_call x1, Pallas kernels, product(): pl.pallas_call(lambda *refs: product_body(rows, cols, *refs), out_shape=j...  7.67 us

profile of v1, /device:TPU:1, one launch (start us, length us, event | category | flops | bytes accessed | tf_op | source)
XLA Modules:
  0.0 108.1 jit_solution(8364771062442056645)
XLA Ops:
  0.0 0.0 copy-start.1
  0.0 0.0 copy-start
  0.0 2.1 %pack.1 = s16[4,128,128]{2,1,0:T(8,128)(2,1)} custom-call(s32[64,64]{1,0:T(8,128)} %refs_0_.1, bf16[256,512]{1,0:T(8,128)(2,1)} %x_ref.1), custom_call_target="tpu_custom_call" | custom-call | tf_op jit(solution)/shard_map/pack/pallas_call | solution.py:34
  2.1 44.8 %all-gather.4 = s16[64,128,128]{2,1,0:T(8,128)(2,1)S(1)} all-gather(s16[4,128,128]{2,1,0:T(8,128)(2,1)} %pack.1), channel_id=2, replica_groups=mesh['row'=32,'col'=16] {'col'}, dimensions={0}, use_global_device_ids=true | all-gather | bytes 2228224 | tf_op jit(solution)/shard_map/all_gather | solution.py:127
  46.9 34.9 %all-gather.5 = s16[128,128,128]{2,1,0:T(8,128)(2,1)S(1)} all-gather(s16[4,128,128]{2,1,0:T(8,128)(2,1)} %pack.1), channel_id=3, replica_groups=mesh['row'=32,'col'=16] {'row'}, dimensions={0}, use_global_device_ids=true | all-gather | bytes 4325376 | tf_op jit(solution)/shard_map/all_gather | solution.py:128
  81.8 0.0 copy-done.1
  81.8 0.0 copy-done
  81.9 7.7 %product.1 = f32[32,16,256]{2,1,0:T(8,128)S(1)} custom-call(s32[64,64]{1,0:T(8,128)S(1)} %copy-done.1, s16[16,4,128,128]{3,2,1,0:T(8,128)(2,1)S(1)} %bitcast.3, s16[32,4,128,128]{3,2,1,0:T(8,128)(2,1)S(1)} %bitcast.2, s32[256,512]{1,0:T(8,128)S(1)} %copy-done), custom_call_target="tpu_custom_call" | custom-call | tf_op jit(solution)/shard_map/product/pallas_call | solution.py:83
  89.5 16.6 %all_to_all.5.x_ref = f32[32,16,256]{2,1,0:T(8,128)} all-to-all(f32[32,16,256]{2,1,0:T(8,128)S(1)} %product.1), channel_id=1, replica_groups=mesh['row'=32,'col'=16] {'row'}, dimensions={0} | all-to-all | bytes 1048576 | tf_op jit(solution)/shard_map/all_to_all | solution.py:130
  106.1 2.0 %scale.1 = f32[1,16,8192]{2,1,0:T(8,128)} custom-call(f32[32,16,256]{2,1,0:T(8,128)} %all_to_all.5.x_ref), custom_call_target="tpu_custom_call" | custom-call | tf_op jit(solution)/shard_map/scale/pallas_call | solution.py:116
Async XLA Ops:
  0.0 81.8 %copy-start.1 = (s32[64,64]{1,0:T(8,128)S(1)}, s32[64,64]{1,0:T(8,128)}, u32[]{:S(2)}) copy-start(s32[64,64]{1,0:T(8,128)} %refs_0_.1) | copy-start | bytes 49156
  0.0 81.8 %copy-start = (s32[256,512]{1,0:T(8,128)S(1)}, s32[256,512]{1,0:T(8,128)}, u32[]{:S(2)}) copy-start(s32[256,512]{1,0:T(8,128)} %refs_3_.1) | copy-start | bytes 1572868

commit v2 on v1

--- a/solution.py
+++ b/solution.py
@@ -8,7 +8,7 @@
 TILE = 128
 LIVE = 4
 UNIT = 16384.0
-STEPS = 4
+X, Y, CORES = 4, 4, 2
 
 
 def spots(rows, cols):
@@ -51,23 +51,24 @@
 
 
 def product_body(rows, cols, live, a_ref, b_ref, keep_ref, out_ref, a_dense, b_dense, total):
-    step = pl.program_id(0)
-    per = a_ref.shape[0]
-    each = b_ref.shape[0] // per
-    top, left = lax.axis_index("row") * rows, lax.axis_index("col") * cols
+    y = pl.program_id(0)
+    place = lax.axis_index("row")
+    top, left = place * rows, lax.axis_index("col") * cols
+    x = place // (Y * CORES)
 
-    @pl.when(step == 0)
+    @pl.when(y == 0)
     def _():
         total[...] = jnp.zeros_like(total)
 
-    for p in range(per):
-        panel = step * per + p
-        unpack(live, top, panel * cols, rows, cols, a_ref, p, a_dense.at[p % 2], 0)
-        for e in range(each):
-            unpack(live, (panel * each + e) * rows, left, rows, cols, b_ref, p * each + e, b_dense.at[p % 2], e * rows * TILE)
-        total[...] += jnp.dot(a_dense[p % 2], b_dense[p % 2], preferred_element_type=jnp.float32)
+    for back in range(X):
+        from_x = lax.rem(x + X - back, X)
+        panel = from_x * Y + y
+        unpack(live, top, panel * cols, rows, cols, a_ref.at[:, 0], from_x, a_dense.at[back % 2], 0)
+        for e in range(CORES):
+            unpack(live, (panel * CORES + e) * rows, left, rows, cols, b_ref.at[:, back, 0], e, b_dense.at[back % 2], e * rows * TILE)
+        total[...] += jnp.dot(a_dense[back % 2], b_dense[back % 2], preferred_element_type=jnp.float32)
 
-    @pl.when(step == pl.num_programs(0) - 1)
+    @pl.when(y == Y - 1)
     def _():
         kept = total[...] * (keep_ref[...].astype(jnp.float32) * (1.0 / (UNIT * UNIT)))
         inflated = (kept * kept).T
@@ -75,22 +76,20 @@
 
 
 def product(tile_live, row_panel, col_panel, keep):
-    n_row, n_col = col_panel.shape[0], row_panel.shape[0]
+    n_row = X * Y * CORES
     height, width = keep.shape
     rows, cols = height // TILE, width // TILE
-    per = n_col // STEPS
-    each = width // height
     return pl.pallas_call(
         lambda *refs: product_body(rows, cols, *refs),
         out_shape=jax.ShapeDtypeStruct((n_row, width // n_row, height), jnp.float32),
-        grid=(STEPS,),
+        grid=(Y,),
         in_specs=[
             pl.BlockSpec(memory_space=pltpu.SMEM),
-            pl.BlockSpec((per, LIVE, TILE, TILE), lambda s: (s, 0, 0, 0)),
-            pl.BlockSpec((per * each, LIVE, TILE, TILE), lambda s: (s, 0, 0, 0)),
-            pl.BlockSpec((height, width), lambda s: (0, 0)),
+            pl.BlockSpec((X, 1, LIVE, TILE, TILE), lambda y: (0, y, 0, 0, 0)),
+            pl.BlockSpec((CORES, X, 1, LIVE, TILE, TILE), lambda y: (0, 0, y, 0, 0, 0)),
+            pl.BlockSpec((height, width), lambda y: (0, 0)),
         ],
-        out_specs=pl.BlockSpec((n_row, width // n_row, height), lambda s: (0, 0, 0)),
+        out_specs=pl.BlockSpec((n_row, width // n_row, height), lambda y: (0, 0, 0)),
         scratch_shapes=[
             pltpu.VMEM((2, height, width), jnp.bfloat16),
             pltpu.VMEM((2, width, width), jnp.bfloat16),
@@ -98,7 +97,7 @@
         ],
         compiler_params=pltpu.CompilerParams(dimension_semantics=("arbitrary",), vmem_limit_bytes=32 * 1024 * 1024),
         name="product",
-    )(tile_live, row_panel, col_panel, keep)
+    )(tile_live, row_panel.reshape(X, Y, LIVE, TILE, TILE), col_panel, keep)
 
 
 def scale_body(x_ref, out_ref):
@@ -122,10 +121,22 @@
     )(entries)
 
 
+def row_place(x, y, core):
+    return (x * Y + y) * CORES + core
+
+
 def shards(transition, tile_live, prune_keep):
+    along_y = [[row_place(x, y, c) for y in range(Y)] for x in range(X) for c in range(CORES)]
+    pairs = [[row_place(x, y, c) for c in range(CORES)] for x in range(X) for y in range(Y)]
+    ahead = [
+        [(row_place(x, y, c), row_place((x + step) % X, y, c)) for x in range(X) for y in range(Y) for c in range(CORES)]
+        for step in range(X)
+    ]
     packed = pack(tile_live, transition)
+    mine = lax.all_gather(packed, "row", axis=0, axis_index_groups=along_y)
+    from_x = [mine] + [lax.ppermute(mine, "row", ahead[step]) for step in range(1, X)]
     row_panel = lax.all_gather(packed, "col", axis=0)
-    col_panel = lax.all_gather(packed, "row", axis=0)
+    col_panel = lax.all_gather(jnp.stack(from_x), "row", axis=0, axis_index_groups=pairs)
     strips = product(tile_live, row_panel, col_panel, prune_keep)
     entries = lax.all_to_all(strips, "row", split_axis=0, concat_axis=0, tiled=True)
     return scale(entries)

time: 108 us -> 110 us (1.019)
  starting transfers between devices: 0 us -> 11.9 us
  blocking collectives: 96.3 us -> 85.2 us
    ppermute x0 -> x3, starting transfers between devices: none -> 11.9 us  [shards(): lax.ppermute(mine, 'row', ahead[step])]
    all_gather x1 -> x2, blocking collectives: 34.9 us -> 23.1 us  [the longest x1 11.7 us: shards(): lax.all_gather(jnp.stack(from_x), 'row', axis=0, axis_index_groups=pairs)]
  transfers between devices with their start and end apart: 0 -> 3, of which waited for: 0 -> 0; matrix products, arithmetic and copies ran while one was open for 0% -> 0% of each run, Pallas kernels for 0% -> 0%
where the time goes in v2:
time: 110 us; the launch traced here: 109 us
  blocking collectives  85.2 us (77%)
  Pallas kernels  12 us (11%)
  starting transfers between devices  11.9 us (11%)
    all_gather x1, blocking collectives, shards(): row_panel = lax.all_gather(packed, 'col', axis=0)  44.9 us
    all_to_all x1, blocking collectives, shards(): lax.all_to_all(strips, 'row', split_axis=0, concat_axis=0, tiled=True)  17.2 us
    ppermute x3, starting transfers between devices, shards(): lax.ppermute(mine, 'row', ahead[step])  11.9 us
    all_gather x1, blocking collectives, shards(): lax.all_gather(jnp.stack(from_x), 'row', axis=0, axis_index_groups=pairs)  11.7 us
    all_gather x1, blocking collectives, shards(): mine = lax.all_gather(packed, 'row', axis=0, axis_index_groups=along_y)  11.4 us
    pallas_call x1, Pallas kernels, product(): pl.pallas_call(lambda *refs: product_body(rows, cols, *refs), out_shape=j...  8.06 us
  transfers between devices with their start and end apart: 3, of which 0 were waited for; matrix products, arithmetic and copies ran while one was open for 0% of the time, Pallas kernels for 0%

profile of v2, /device:TPU:1, one launch (start us, length us, event | category | flops | bytes accessed | tf_op | source)
XLA Modules:
  0.0 109.4 jit_solution(3092547551598385094)
XLA Ops:
  0.0 2.0 %pack.1 = s16[4,128,128]{2,1,0:T(8,128)(2,1)} custom-call(s32[64,64]{1,0:T(8,128)} %refs_0_.1, bf16[256,512]{1,0:T(8,128)(2,1)} %x_ref.1), custom_call_target="tpu_custom_call" | custom-call | tf_op jit(solution)/shard_map/pack/pallas_call | solution.py:34
  2.0 11.4 %all-gather.1 = s16[16,128,128]{2,1,0:T(8,128)(2,1)S(1)} all-gather(s16[4,128,128]{2,1,0:T(8,128)(2,1)} %pack.1), channel_id=3, replica_groups={{0,32,64,96},{16,48,80,112},{128,160,192,224},{144,176,208,240},{256,28..., dimensions={0}, use_global_device_ids=true | all-gather | bytes 655360 | tf_op jit(solution)/shard_map/all_gather | solution.py:136
  13.4 4.5 %collective-permute-start = (s16[4,4,128,128]{3,2,1,0:T(8,128)(2,1)S(1)}, s16[4,4,128,128]{3,2,1,0:T(8,128)(2,1)S(1)}, u32[]{:S(2)}, u32[]{:S(2)}) collective-permute-start(s16[4,4,128,128]{3,2,1,0:T(8,128)(2,1)S(1)} %bitcast.9), channel_id=1, source_target_pairs={{0,128},{16,144},{32,160},{48,176},{64,192},{80,208},{96,224},{112... | collective-permute-start | bytes 1572872 | tf_op jit(solution)/shard_map/ppermute | solution.py:137
  17.9 4.3 %collective-permute-start.1 = (s16[4,4,128,128]{3,2,1,0:T(8,128)(2,1)S(1)}, s16[4,4,128,128]{3,2,1,0:T(8,128)(2,1)S(1)}, u32[]{:S(2)}, u32[]{:S(2)}) collective-permute-start(s16[4,4,128,128]{3,2,1,0:T(8,128)(2,1)S(1)} %bitcast.10), channel_id=1, source_target_pairs={{0,256},{16,272},{32,288},{48,304},{64,320},{80,336},{96,352},{112... | collective-permute-start | bytes 1572872 | tf_op jit(solution)/shard_map/ppermute | solution.py:137
  22.3 3.1 %collective-permute-start.2 = (s16[4,4,128,128]{3,2,1,0:T(8,128)(2,1)S(1)}, s16[4,4,128,128]{3,2,1,0:T(8,128)(2,1)S(1)}, u32[]{:S(2)}, u32[]{:S(2)}) collective-permute-start(s16[4,4,128,128]{3,2,1,0:T(8,128)(2,1)S(1)} %bitcast.11), channel_id=1, source_target_pairs={{0,384},{16,400},{32,416},{48,432},{64,448},{80,464},{96,480},{112... | collective-permute-start | bytes 1572872 | tf_op jit(solution)/shard_map/ppermute | solution.py:137
  25.3 44.9 %all-gather.6 = s16[64,128,128]{2,1,0:T(8,128)(2,1)S(1)} all-gather(s16[4,128,128]{2,1,0:T(8,128)(2,1)} %pack.1), channel_id=2, replica_groups=mesh['row'=32,'col'=16] {'col'}, dimensions={0}, use_global_device_ids=true | all-gather | bytes 2228224 | tf_op jit(solution)/shard_map/all_gather | solution.py:138
  70.2 0.0 collective-permute-done
  70.3 0.0 collective-permute-done.1
  70.3 0.0 collective-permute-done.2
  70.3 0.2 pad_add_fusion
  70.5 0.0 copy-start
  70.5 0.0 copy-start.1
  70.5 11.7 %all-gather.5 = s16[8,4,4,128,128]{4,3,2,1,0:T(8,128)(2,1)S(1)} all-gather(s16[4,4,4,128,128]{4,3,2,1,0:T(8,128)(2,1)S(1)} %pad_add_fusion), channel_id=4, replica_groups={{0,16},{32,48},{64,80},{96,112},{128,144},{160,176},{192,208},{224,240}..., dimensions={0}, use_global_device_ids=true | all-gather | bytes 6291456 | tf_op jit(solution)/shard_map/all_gather | solution.py:139
  82.2 0.0 copy-done
  82.2 0.0 copy-done.1
  82.2 8.1 %product.1 = f32[32,16,256]{2,1,0:T(8,128)S(1)} custom-call(s32[64,64]{1,0:T(8,128)S(1)} %copy-done.1, s16[4,4,4,128,128]{4,3,2,1,0:T(8,128)(2,1)S(1)} %bitcast.8, s16[2,4,4,4,128,128]{5,4,3,2,1,0:T(8,128)(2,1)S(1)} %bitcast.7, s32[256,512]{1,0:T(8,128)S(1)} %copy-done), custom_call_target="tpu_custom_call" | custom-call | tf_op jit(solution)/shard_map/product/pallas_call | solution.py:82
  90.2 17.2 %all_to_all.5.x_ref = f32[32,16,256]{2,1,0:T(8,128)} all-to-all(f32[32,16,256]{2,1,0:T(8,128)S(1)} %product.1), channel_id=1, replica_groups=mesh['row'=32,'col'=16] {'row'}, dimensions={0} | all-to-all | bytes 1048576 | tf_op jit(solution)/shard_map/all_to_all | solution.py:141
  107.4 2.0 %scale.1 = f32[1,16,8192]{2,1,0:T(8,128)} custom-call(f32[32,16,256]{2,1,0:T(8,128)} %all_to_all.5.x_ref), custom_call_target="tpu_custom_call" | custom-call | tf_op jit(solution)/shard_map/scale/pallas_call | solution.py:115
Async XLA Ops:
  13.4 56.8 %collective-permute-start = (s16[4,4,128,128]{3,2,1,0:T(8,128)(2,1)S(1)}, s16[4,4,128,128]{3,2,1,0:T(8,128)(2,1)S(1)}, u32[]{:S(2)}, u32[]{:S(2)}) collective-permute-start(s16[4,4,128,128]{3,2,1,0:T(8,128)(2,1)S(1)} %bitcast.9), channel_id=1, source_target_pairs={{0,128},{16,144},{32,160},{48,176},{64,192},{80,208},{96,224},{112... | collective-permute-start | bytes 1572872 | tf_op jit(solution)/shard_map/ppermute | solution.py:137
  17.9 52.3 %collective-permute-start.1 = (s16[4,4,128,128]{3,2,1,0:T(8,128)(2,1)S(1)}, s16[4,4,128,128]{3,2,1,0:T(8,128)(2,1)S(1)}, u32[]{:S(2)}, u32[]{:S(2)}) collective-permute-start(s16[4,4,128,128]{3,2,1,0:T(8,128)(2,1)S(1)} %bitcast.10), channel_id=1, source_target_pairs={{0,256},{16,272},{32,288},{48,304},{64,320},{80,336},{96,352},{112... | collective-permute-start | bytes 1572872 | tf_op jit(solution)/shard_map/ppermute | solution.py:137
  22.3 48.0 %collective-permute-start.2 = (s16[4,4,128,128]{3,2,1,0:T(8,128)(2,1)S(1)}, s16[4,4,128,128]{3,2,1,0:T(8,128)(2,1)S(1)}, u32[]{:S(2)}, u32[]{:S(2)}) collective-permute-start(s16[4,4,128,128]{3,2,1,0:T(8,128)(2,1)S(1)} %bitcast.11), channel_id=1, source_target_pairs={{0,384},{16,400},{32,416},{48,432},{64,448},{80,464},{96,480},{112... | collective-permute-start | bytes 1572872 | tf_op jit(solution)/shard_map/ppermute | solution.py:137
  70.5 11.7 %copy-start = (s32[256,512]{1,0:T(8,128)S(1)}, s32[256,512]{1,0:T(8,128)}, u32[]{:S(2)}) copy-start(s32[256,512]{1,0:T(8,128)} %refs_3_.1) | copy-start | bytes 1572868
  70.5 11.7 %copy-start.1 = (s32[64,64]{1,0:T(8,128)S(1)}, s32[64,64]{1,0:T(8,128)}, u32[]{:S(2)}) copy-start(s32[64,64]{1,0:T(8,128)} %refs_0_.1) | copy-start | bytes 49156

commit v3 on v2

v3 whole, which is shorter than its diff:
```python
import jax
import jax.numpy as jnp
from jax import lax
from jax.experimental import pallas as pl
from jax.experimental.pallas import tpu as pltpu
from jax.sharding import PartitionSpec as P

TILE = 128
LIVE = 4
UNIT = 16384.0
X, Y, CORES = 4, 4, 2


def spots(rows, cols):
    half = cols // CORES
    return [(a, side * half + b) for side in range(CORES) for a in range(rows) for b in range(half)]


def tile_at(a, b):
    return slice(a * TILE, (a + 1) * TILE), slice(b * TILE, (b + 1) * TILE)


def pack_body(live, x_ref, out_ref):
    rows, cols = x_ref.shape[0] // TILE, x_ref.shape[1] // TILE
    top, left = lax.axis_index("row") * rows, lax.axis_index("col") * cols
    slot = jnp.int32(0)
    for a, b in spots(rows, cols):
        flag = live[top + a, left + b]

        @pl.when((flag > 0) & (slot < LIVE))
        def _(slot=slot, a=a, b=b):
            units = x_ref[tile_at(a, b)].astype(jnp.float32) * UNIT
            out_ref[slot] = units.astype(jnp.int32).astype(jnp.int16)

        slot = slot + flag


def pack(tile_live, transition):
    return pl.pallas_call(
        pack_body,
        out_shape=jax.ShapeDtypeStruct((LIVE, TILE, TILE), jnp.int16),
        in_specs=[pl.BlockSpec(memory_space=pltpu.SMEM), pl.BlockSpec(memory_space=pltpu.VMEM)],
        out_specs=pl.BlockSpec(memory_space=pltpu.VMEM),
        name="pack",
    )(tile_live, transition)


def unpack(live, top, left, places, slots_ref, slot, dense_ref, down, across):
    for a, b in places:
        flag = live[top + a, left + b]
        tile = slots_ref[jnp.minimum(slot, LIVE - 1)].astype(jnp.float32)
        tile = jnp.where(flag > 0, tile, 0.0).astype(jnp.bfloat16)
        dense_ref[down + a * TILE : down + (a + 1) * TILE, across + b * TILE : across + (b + 1) * TILE] = tile
        slot = slot + flag


def half_body(other, rows, cols, live, a_ref, b_ref, *refs):
    if other:
        before_ref, keep_ref, out_ref, a_dense, b_dense, total = refs
    else:
        out_ref, a_dense, b_dense = refs
        total = out_ref
    place = lax.axis_index("row")
    top, left = place * rows, lax.axis_index("col") * cols
    x, y = place // (Y * CORES), lax.rem(place // CORES, Y)
    side = lax.rem(place, CORES)
    if other:
        side = 1 - side
    half = cols // CORES
    total[...] = before_ref[...] if other else jnp.zeros_like(total)

    @pl.loop(0, X)
    def _(back_x):
        for back_y in range(Y):
            panel = lax.rem(x + X - back_x, X) * Y + lax.rem(y + Y - back_y, Y)
            first = sum(live[top + a, panel * cols + b] for a in range(rows) for b in range(half))
            unpack(
                live, top, panel * cols + side * half, [(a, b) for a in range(rows) for b in range(half)],
                a_ref.at[panel], side * first, a_dense, 0, back_y * half * TILE,
            )
            unpack(
                live, (panel * CORES + side) * rows, left, spots(rows, cols),
                b_ref.at[back_x, back_y], jnp.int32(0), b_dense, back_y * rows * TILE, 0,
            )
        total[...] += jnp.dot(a_dense[...], b_dense[...], preferred_element_type=jnp.float32)

    if other:
        kept = total[...] * (keep_ref[...].astype(jnp.float32) * (1.0 / (UNIT * UNIT)))
        inflated = (kept * kept).T
        out_ref[...] = inflated.reshape(out_ref.shape)


def half_product(tile_live, row_panel, col_half, *rest):
    n_row = X * Y * CORES
    height, width = TILE * tile_live.shape[0] // n_row, TILE * tile_live.shape[1] // row_panel.shape[0]
    rows, cols = height // TILE, width // TILE
    other = bool(rest)
    out = (n_row, width // n_row, height) if other else (height, width)
    depth = Y * height
    in_vmem = pl.BlockSpec(memory_space=pltpu.VMEM)
    return pl.pallas_call(
        lambda *refs: half_body(other, rows, cols, *refs),
        out_shape=jax.ShapeDtypeStruct(out, jnp.float32),
        in_specs=[pl.BlockSpec(memory_space=pltpu.SMEM), in_vmem, in_vmem, *[in_vmem for _ in rest]],
        out_specs=in_vmem,
        scratch_shapes=[
            pltpu.VMEM((height, depth), jnp.bfloat16),
            pltpu.VMEM((depth, width), jnp.bfloat16),
        ] + [pltpu.VMEM((height, width), jnp.float32)] * other,
        compiler_params=pltpu.CompilerParams(vmem_limit_bytes=24 * 1024 * 1024),
        cost_estimate=pl.CostEstimate(flops=2 * height * depth * X * width, bytes_accessed=5 * 1024 * 1024, transcendentals=0),
        name="other_half" if other else "own_half",
    )(tile_live, row_panel, col_half, *rest)


def scale_body(x_ref, out_ref):
    parts, _, height = x_ref.shape
    nodes = parts * height
    entries = x_ref[...]
    column_total = jnp.sum(jnp.sum(entries, axis=0), axis=1, keepdims=True)
    factor = nodes / column_total
    for p in range(parts):
        out_ref[0, :, p * height : (p + 1) * height] = entries[p] * factor


def scale(entries):
    parts, strips, height = entries.shape
    return pl.pallas_call(
        scale_body,
        out_shape=jax.ShapeDtypeStruct((1, strips, parts * height), jnp.float32),
        in_specs=[pl.BlockSpec(memory_space=pltpu.VMEM)],
        out_specs=pl.BlockSpec(memory_space=pltpu.VMEM),
        name="scale",
    )(entries)


def row_place(x, y, core):
    return (x % X * Y + y % Y) * CORES + core % CORES


def moved(part, x=0, y=0, core=0):
    hops = [
        (row_place(i, j, k), row_place(i + x, j + y, k + core)) for i in range(X) for j in range(Y) for k in range(CORES)
    ]
    return lax.ppermute(part, "row", hops)


def shards(transition, tile_live, prune_keep):
    packed = pack(tile_live, transition)
    around = jnp.stack([packed] + [moved(packed, y=step) for step in range(1, Y)])
    own = [around] + [moved(around, x=step) for step in range(1, X)]
    row_panel = lax.all_gather(packed, "col", axis=0)
    own = jnp.stack(own) + jnp.minimum(row_panel[0, 0, 0, 0], 0)
    other = moved(own, core=1)
    total = half_product(tile_live, row_panel, own)
    strips = half_product(tile_live, row_panel, other, total, prune_keep)
    entries = lax.all_to_all(strips, "row", split_axis=0, concat_axis=0, tiled=True)
    return scale(entries)


def solution(mesh):
    placed = (P("row", "col"), P(), P("row", "col"))
    return jax.shard_map(
        shards, mesh=mesh, in_specs=placed, out_specs=P("col", "row", None), check_vma=False
    )
```

time: 110 us -> 112 us (1.018)
  blocking collectives: 85.2 us -> 59.9 us
  starting transfers between devices: 11.9 us -> 31.3 us
  waiting for transfers between devices: 0.01 us -> 4.51 us
  other arithmetic: 0.21 us -> 1.72 us
    all_gather x2 -> x0, blocking collectives: 23.1 us -> none  [the longest x1 11.7 us: shards(): lax.all_gather(jnp.stack(from_x), 'row', axis=0, axis_index_groups=pairs)]
    ppermute x3 -> x7, starting transfers between devices: 11.9 us -> 31.3 us  [moved(): return lax.ppermute(part, 'row', hops)]
    ppermute x3 -> x7, waiting for transfers between devices: 0.01 us -> 4.51 us  [moved(): return lax.ppermute(part, 'row', hops)]
    all_to_all x1, blocking collectives: 17.2 us -> 15.5 us  [shards(): lax.all_to_all(strips, 'row', split_axis=0, concat_axis=0, tiled=True)]
    pallas_call x1 -> x2, Pallas kernels: 8.06 us -> 8.49 us  [half_product(): pl.pallas_call(lambda *refs: half_body(other, rows, cols, *refs), out_sha...]
  transfers between devices with their start and end apart: 3 -> 7, of which waited for: 0 -> 2; matrix products, arithmetic and copies ran while one was open for 0% -> 0% of each run, Pallas kernels for 0% -> 4%
where the time goes in v3:
time: 112 us; the launch traced here: 111 us
  blocking collectives  59.9 us (53%)
  starting transfers between devices  31.3 us (28%)
  Pallas kernels  12.4 us (11%)
  waiting for transfers between devices  4.51 us (4%)
  other arithmetic  1.72 us (2%)
    all_gather x1, blocking collectives, shards(): row_panel = lax.all_gather(packed, 'col', axis=0)  44.5 us
    ppermute x7, starting transfers between devices, moved(): return lax.ppermute(part, 'row', hops)  31.3 us
    all_to_all x1, blocking collectives, shards(): lax.all_to_all(strips, 'row', split_axis=0, concat_axis=0, tiled=True)  15.5 us
    pallas_call x2, Pallas kernels, half_product(): pl.pallas_call(lambda *refs: half_body(other, rows, cols, *refs), out_sha...  8.49 us
    ppermute x7, waiting for transfers between devices, moved(): return lax.ppermute(part, 'row', hops)  4.51 us
  transfers between devices with their start and end apart: 7, of which 2 were waited for; matrix products, arithmetic and copies ran while one was open for 0% of the time, Pallas kernels for 4%

profile of v3, /device:TPU:1, one launch (start us, length us, event | category | flops | bytes accessed | tf_op | source)
XLA Modules:
  0.0 111.3 jit_solution(1898237088705214229)
XLA Ops:
  0.0 2.0 %pack.1 = s16[4,128,128]{2,1,0:T(8,128)(2,1)} custom-call(s32[64,64]{1,0:T(8,128)} %refs_0_.3, bf16[256,512]{1,0:T(8,128)(2,1)} %x_ref.1), custom_call_target="tpu_custom_call" | custom-call | tf_op jit(solution)/shard_map/pack/pallas_call | solution.py:39
  2.0 5.5 %collective-permute-start.2 = (s16[4,128,128]{2,1,0:T(8,128)(2,1)}, s16[4,128,128]{2,1,0:T(8,128)(2,1)S(1)}, u32[]{:S(2)}, u32[]{:S(2)}) collective-permute-start(s16[4,128,128]{2,1,0:T(8,128)(2,1)} %pack.1), channel_id=1, source_target_pairs={{0,96},{16,112},{32,0},{48,16},{64,32},{80,48},{96,64},{112,80},{1... | collective-permute-start | bytes 393224 | tf_op jit(solution)/shard_map/ppermute | solution.py:145
  7.4 2.3 %collective-permute-start.1 = (s16[4,128,128]{2,1,0:T(8,128)(2,1)}, s16[4,128,128]{2,1,0:T(8,128)(2,1)S(1)}, u32[]{:S(2)}, u32[]{:S(2)}) collective-permute-start(s16[4,128,128]{2,1,0:T(8,128)(2,1)} %pack.1), channel_id=1, source_target_pairs={{0,64},{16,80},{32,96},{48,112},{64,0},{80,16},{96,32},{112,48},{1... | collective-permute-start | bytes 393224 | tf_op jit(solution)/shard_map/ppermute | solution.py:145
  9.7 2.6 %collective-permute-start = (s16[4,128,128]{2,1,0:T(8,128)(2,1)}, s16[4,128,128]{2,1,0:T(8,128)(2,1)S(1)}, u32[]{:S(2)}, u32[]{:S(2)}) collective-permute-start(s16[4,128,128]{2,1,0:T(8,128)(2,1)} %pack.1), channel_id=1, source_target_pairs={{0,32},{16,48},{32,64},{48,80},{64,96},{80,112},{96,0},{112,16},{1... | collective-permute-start | bytes 393224 | tf_op jit(solution)/shard_map/ppermute | solution.py:145
  12.3 0.0 collective-permute-done.2
  12.3 2.5 %collective-permute-done.1 = s16[4,128,128]{2,1,0:T(8,128)(2,1)S(1)} collective-permute-done((s16[4,128,128]{2,1,0:T(8,128)(2,1)}, s16[4,128,128]{2,1,0:T(8,128)(2,1)S(1)}, u32[]{:S(2)}, u32[]{:S(2)}) %collective-permute-start.1) | collective-permute-done | bytes 131104 | tf_op jit(solution)/shard_map/ppermute | solution.py:145
  14.9 2.0 %collective-permute-done = s16[4,128,128]{2,1,0:T(8,128)(2,1)S(1)} collective-permute-done((s16[4,128,128]{2,1,0:T(8,128)(2,1)}, s16[4,128,128]{2,1,0:T(8,128)(2,1)S(1)}, u32[]{:S(2)}, u32[]{:S(2)}) %collective-permute-start) | collective-permute-done | bytes 131104 | tf_op jit(solution)/shard_map/ppermute | solution.py:145
  16.8 1.1 %fusion = (s16[1,4,4,128,128]{4,3,2,1,0:T(8,128)(2,1)S(1)}, s16[4,4,128,128]{3,2,1,0:T(8,128)(2,1)S(1)}) fusion(s16[1,4,128,128]{3,2,1,0:T(8,128)(2,1)S(1)} %bitcast.18, s16[1,4,128,128]{3,2,1,0:T(8,128)(2,1)S(1)} %bitcast.19, s16[1,4,128,128]{3,2,1,0:T(8,128)(2,1)S(1)} %bitcast.20, s16[1,4,128,128]{3,2,1,0:T(8,128)(2,1)} %bitcast.14), kind=kLoop, calls=%fused_computation.2 | loop fusion | flops 786432 | bytes 1572864 | tf_op jit(solution)/shard_map/stack | solution.py:153
  18.0 6.0 %collective-permute-start.5 = (s16[4,4,128,128]{3,2,1,0:T(8,128)(2,1)S(1)}, s16[4,4,128,128]{3,2,1,0:T(8,128)(2,1)S(1)}, u32[]{:S(2)}, u32[]{:S(2)}) collective-permute-start(s16[4,4,128,128]{3,2,1,0:T(8,128)(2,1)S(1)} %get-tuple-element.6), channel_id=1, source_target_pairs={{0,384},{16,400},{32,416},{48,432},{64,448},{80,464},{96,480},{112... | collective-permute-start | bytes 1572872 | tf_op jit(solution)/shard_map/ppermute | solution.py:145
  24.0 2.5 %collective-permute-start.4 = (s16[4,4,128,128]{3,2,1,0:T(8,128)(2,1)S(1)}, s16[4,4,128,128]{3,2,1,0:T(8,128)(2,1)S(1)}, u32[]{:S(2)}, u32[]{:S(2)}) collective-permute-start(s16[4,4,128,128]{3,2,1,0:T(8,128)(2,1)S(1)} %get-tuple-element.6), channel_id=1, source_target_pairs={{0,256},{16,272},{32,288},{48,304},{64,320},{80,336},{96,352},{112... | collective-permute-start | bytes 1572872 | tf_op jit(solution)/shard_map/ppermute | solution.py:145
  26.5 2.5 %collective-permute-start.3 = (s16[4,4,128,128]{3,2,1,0:T(8,128)(2,1)S(1)}, s16[4,4,128,128]{3,2,1,0:T(8,128)(2,1)S(1)}, u32[]{:S(2)}, u32[]{:S(2)}) collective-permute-start(s16[4,4,128,128]{3,2,1,0:T(8,128)(2,1)S(1)} %get-tuple-element.6), channel_id=1, source_target_pairs={{0,128},{16,144},{32,160},{48,176},{64,192},{80,208},{96,224},{112... | collective-permute-start | bytes 1572872 | tf_op jit(solution)/shard_map/ppermute | solution.py:145
  29.0 44.5 %all-gather.2 = s16[64,128,128]{2,1,0:T(8,128)(2,1)S(1)} all-gather(s16[4,128,128]{2,1,0:T(8,128)(2,1)} %pack.1), channel_id=2, replica_groups=mesh['row'=32,'col'=16] {'col'}, dimensions={0}, use_global_device_ids=true | all-gather | bytes 2228224 | tf_op jit(solution)/shard_map/all_gather | solution.py:152
  73.4 0.5 slice.4
  74.6 0.0 collective-permute-done.5
  74.6 0.0 collective-permute-done.4
  74.6 0.0 collective-permute-done.3
  74.6 0.0 copy-start.1
  74.7 0.6 add_add_fusion.refs_2_
  75.3 0.0 copy-start
  75.3 10.0 %collective-permute-start.6 = (s16[4,4,4,128,128]{4,3,2,1,0:T(8,128)(2,1)S(1)}, s16[4,4,4,128,128]{4,3,2,1,0:T(8,128)(2,1)S(1)}, u32[]{:S(2)}, u32[]{:S(2)}) collective-permute-start(s16[4,4,4,128,128]{4,3,2,1,0:T(8,128)(2,1)S(1)} %add_add_fusion.refs_2_), channel_id=1, source_target_pairs={{0,16},{16,0},{32,48},{48,32},{64,80},{80,64},{96,112},{112,96},{1... | collective-permute-start | bytes 6291464 | tf_op jit(solution)/shard_map/ppermute | solution.py:145
  85.3 0.0 copy-done.1
  85.3 4.2 %own_half.1.refs_3_ = f32[256,512]{1,0:T(8,128)S(1)} custom-call(s32[64,64]{1,0:T(8,128)S(1)} %copy-done.1, s16[16,4,128,128]{3,2,1,0:T(8,128)(2,1)S(1)} %bitcast.12, s16[4,4,4,128,128]{4,3,2,1,0:T(8,128)(2,1)S(1)} %add_add_fusion.refs_2_), custom_call_target="tpu_custom_call" | custom-call | flops 1073741824 | bytes 5242880 | tf_op jit(solution)/shard_map/own_half/pallas_call | solution.py:101
  89.5 0.0 collective-permute-done.6.refs_2_
  89.5 0.0 copy-done
  89.5 4.3 %other_half.1 = f32[32,16,256]{2,1,0:T(8,128)S(1)} custom-call(s32[64,64]{1,0:T(8,128)S(1)} %copy-done.1, s16[16,4,128,128]{3,2,1,0:T(8,128)(2,1)S(1)} %bitcast.13, s16[4,4,4,128,128]{4,3,2,1,0:T(8,128)(2,1)S(1)} %collective-permute-done.6.refs_2_, f32[256,512]{1,0:T(8,128)S(1)} %own_half.1.refs_3_, s32[256,512]{1,0:T(8,128)S(1)} %copy-done), custom_call_target="tpu_custom_call" | custom-call | flops 1073741824 | bytes 5242880 | tf_op jit(solution)/shard_map/other_half/pallas_call | solution.py:101
  93.8 15.5 %all_to_all.5.x_ref = f32[32,16,256]{2,1,0:T(8,128)} all-to-all(f32[32,16,256]{2,1,0:T(8,128)S(1)} %other_half.1), channel_id=1, replica_groups=mesh['row'=32,'col'=16] {'row'}, dimensions={0} | all-to-all | bytes 1048576 | tf_op jit(solution)/shard_map/all_to_all | solution.py:157
  109.3 2.0 %scale.1 = f32[1,16,8192]{2,1,0:T(8,128)} custom-call(f32[32,16,256]{2,1,0:T(8,128)} %all_to_all.5.x_ref), custom_call_target="tpu_custom_call" | custom-call | tf_op jit(solution)/shard_map/scale/pallas_call | solution.py:128
Async XLA Ops:
  2.0 10.4 %collective-permute-start.2 = (s16[4,128,128]{2,1,0:T(8,128)(2,1)}, s16[4,128,128]{2,1,0:T(8,128)(2,1)S(1)}, u32[]{:S(2)}, u32[]{:S(2)}) collective-permute-start(s16[4,128,128]{2,1,0:T(8,128)(2,1)} %pack.1), channel_id=1, source_target_pairs={{0,96},{16,112},{32,0},{48,16},{64,32},{80,48},{96,64},{112,80},{1... | collective-permute-start | bytes 393224 | tf_op jit(solution)/shard_map/ppermute | solution.py:145
  7.4 7.4 %collective-permute-start.1 = (s16[4,128,128]{2,1,0:T(8,128)(2,1)}, s16[4,128,128]{2,1,0:T(8,128)(2,1)S(1)}, u32[]{:S(2)}, u32[]{:S(2)}) collective-permute-start(s16[4,128,128]{2,1,0:T(8,128)(2,1)} %pack.1), channel_id=1, source_target_pairs={{0,64},{16,80},{32,96},{48,112},{64,0},{80,16},{96,32},{112,48},{1... | collective-permute-start | bytes 393224 | tf_op jit(solution)/shard_map/ppermute | solution.py:145
  9.7 7.1 %collective-permute-start = (s16[4,128,128]{2,1,0:T(8,128)(2,1)}, s16[4,128,128]{2,1,0:T(8,128)(2,1)S(1)}, u32[]{:S(2)}, u32[]{:S(2)}) collective-permute-start(s16[4,128,128]{2,1,0:T(8,128)(2,1)} %pack.1), channel_id=1, source_target_pairs={{0,32},{16,48},{32,64},{48,80},{64,96},{80,112},{96,0},{112,16},{1... | collective-permute-start | bytes 393224 | tf_op jit(solution)/shard_map/ppermute | solution.py:145
  18.0 56.6 %collective-permute-start.5 = (s16[4,4,128,128]{3,2,1,0:T(8,128)(2,1)S(1)}, s16[4,4,128,128]{3,2,1,0:T(8,128)(2,1)S(1)}, u32[]{:S(2)}, u32[]{:S(2)}) collective-permute-start(s16[4,4,128,128]{3,2,1,0:T(8,128)(2,1)S(1)} %get-tuple-element.6), channel_id=1, source_target_pairs={{0,384},{16,400},{32,416},{48,432},{64,448},{80,464},{96,480},{112... | collective-permute-start | bytes 1572872 | tf_op jit(solution)/shard_map/ppermute | solution.py:145
  24.0 50.6 %collective-permute-start.4 = (s16[4,4,128,128]{3,2,1,0:T(8,128)(2,1)S(1)}, s16[4,4,128,128]{3,2,1,0:T(8,128)(2,1)S(1)}, u32[]{:S(2)}, u32[]{:S(2)}) collective-permute-start(s16[4,4,128,128]{3,2,1,0:T(8,128)(2,1)S(1)} %get-tuple-element.6), channel_id=1, source_target_pairs={{0,256},{16,272},{32,288},{48,304},{64,320},{80,336},{96,352},{112... | collective-permute-start | bytes 1572872 | tf_op jit(solution)/shard_map/ppermute | solution.py:145
  26.5 48.2 %collective-permute-start.3 = (s16[4,4,128,128]{3,2,1,0:T(8,128)(2,1)S(1)}, s16[4,4,128,128]{3,2,1,0:T(8,128)(2,1)S(1)}, u32[]{:S(2)}, u32[]{:S(2)}) collective-permute-start(s16[4,4,128,128]{3,2,1,0:T(8,128)(2,1)S(1)} %get-tuple-element.6), channel_id=1, source_target_pairs={{0,128},{16,144},{32,160},{48,176},{64,192},{80,208},{96,224},{112... | collective-permute-start | bytes 1572872 | tf_op jit(solution)/shard_map/ppermute | solution.py:145
  74.6 10.6 %copy-start.1 = (s32[64,64]{1,0:T(8,128)S(1)}, s32[64,64]{1,0:T(8,128)}, u32[]{:S(2)}) copy-start(s32[64,64]{1,0:T(8,128)} %refs_0_.3) | copy-start | bytes 49156
  75.3 14.2 %copy-start = (s32[256,512]{1,0:T(8,128)S(1)}, s32[256,512]{1,0:T(8,128)}, u32[]{:S(2)}) copy-start(s32[256,512]{1,0:T(8,128)} %refs_4_.1) | copy-start | bytes 1572868
  75.3 14.2 %collective-permute-start.6 = (s16[4,4,4,128,128]{4,3,2,1,0:T(8,128)(2,1)S(1)}, s16[4,4,4,128,128]{4,3,2,1,0:T(8,128)(2,1)S(1)}, u32[]{:S(2)}, u32[]{:S(2)}) collective-permute-start(s16[4,4,4,128,128]{4,3,2,1,0:T(8,128)(2,1)S(1)} %add_add_fusion.refs_2_), channel_id=1, source_target_pairs={{0,16},{16,0},{32,48},{48,32},{64,80},{80,64},{96,112},{112,96},{1... | collective-permute-start | bytes 6291464 | tf_op jit(solution)/shard_map/ppermute | solution.py:145

commit v4 on v1

v4 whole, which is shorter than its diff:
```python
import jax
import jax.numpy as jnp
from jax import lax
from jax.experimental import pallas as pl
from jax.experimental.pallas import tpu as pltpu
from jax.sharding import PartitionSpec as P

TILE = 128
LIVE = 4
UNIT = 16384.0
STEPS = 4


def spots(rows, cols):
    return [(a, b, slice(a * TILE, (a + 1) * TILE), slice(b * TILE, (b + 1) * TILE)) for a in range(rows) for b in range(cols)]


def pack_body(live, x_ref, units_ref, plain_ref):
    rows, cols = x_ref.shape[0] // TILE, x_ref.shape[1] // TILE
    top, left = lax.axis_index("row") * rows, lax.axis_index("col") * cols
    slot = jnp.int32(0)
    for a, b, across, down in spots(rows, cols):
        flag = live[top + a, left + b]

        @pl.when((flag > 0) & (slot < LIVE))
        def _(slot=slot, across=across, down=down):
            tile = x_ref[across, down]
            plain_ref[slot] = tile
            units_ref[slot] = (tile.astype(jnp.float32) * UNIT).astype(jnp.int32).astype(jnp.int16)

        slot = slot + flag


def pack(tile_live, transition):
    in_vmem = pl.BlockSpec(memory_space=pltpu.VMEM)
    slots = (LIVE, TILE, TILE)
    return pl.pallas_call(
        pack_body,
        out_shape=[jax.ShapeDtypeStruct(slots, jnp.int16), jax.ShapeDtypeStruct(slots, transition.dtype)],
        in_specs=[pl.BlockSpec(memory_space=pltpu.SMEM), in_vmem],
        out_specs=[in_vmem, in_vmem],
        name="pack",
    )(tile_live, transition)


def unpack(live, top, left, rows, cols, slots_ref, group, dense_ref, height, width):
    slot = jnp.int32(0)
    for a, b, _, _ in spots(rows, cols):
        flag = live[top + a, left + b]
        tile = slots_ref[group, jnp.minimum(slot, LIVE - 1)]
        tile = jnp.where(flag > 0, tile, jnp.zeros_like(tile))
        if tile.dtype != dense_ref.dtype:
            tile = tile.astype(jnp.float32).astype(dense_ref.dtype)
        dense_ref[height + a * TILE : height + (a + 1) * TILE, width + b * TILE : width + (b + 1) * TILE] = tile
        slot = slot + flag


def spread_body(rows, cols, live, a_ref, out_ref):
    step = pl.program_id(0)
    per = a_ref.shape[0]
    top = lax.axis_index("row") * rows
    for p in range(per):
        unpack(live, top, (step * per + p) * cols, rows, cols, a_ref, p, out_ref.at[0], 0, p * cols * TILE)


def spread(tile_live, row_panel, height, width):
    per = row_panel.shape[0] // STEPS
    rows, cols = height // TILE, width // TILE
    return pl.pallas_call(
        lambda *refs: spread_body(rows, cols, *refs),
        out_shape=jax.ShapeDtypeStruct((STEPS, height, per * width), jnp.bfloat16),
        grid=(STEPS,),
        in_specs=[
            pl.BlockSpec(memory_space=pltpu.SMEM),
            pl.BlockSpec((per, LIVE, TILE, TILE), lambda s: (s, 0, 0, 0)),
        ],
        out_specs=pl.BlockSpec((1, height, per * width), lambda s: (s, 0, 0)),
        cost_estimate=pl.CostEstimate(flops=0, bytes_accessed=6 * 1024 * 1024, transcendentals=0),
        name="spread",
    )(tile_live, row_panel)


def product_body(rows, cols, live, a_ref, b_ref, keep_ref, out_ref, b_dense, total):
    step = pl.program_id(0)
    per = b_ref.shape[0]
    left = lax.axis_index("col") * cols
    for p in range(per):
        unpack(live, (step * per + p) * rows, left, rows, cols, b_ref, p, b_dense, p * rows * TILE, 0)
    part = jnp.dot(a_ref[0], b_dense[...], preferred_element_type=jnp.float32)

    @pl.when(step == 0)
    def _():
        total[...] = part

    @pl.when(step > 0)
    def _():
        total[...] += part

    @pl.when(step == pl.num_programs(0) - 1)
    def _():
        kept = total[...] * (keep_ref[...].astype(jnp.float32) * (1.0 / UNIT))
        inflated = (kept * kept).T
        out_ref[...] = inflated.reshape(out_ref.shape)


def product(tile_live, row_panel, col_panel, keep):
    n_row, depth = col_panel.shape[0], row_panel.shape[2]
    height, width = keep.shape
    rows, cols = height // TILE, width // TILE
    return pl.pallas_call(
        lambda *refs: product_body(rows, cols, *refs),
        out_shape=jax.ShapeDtypeStruct((n_row, width // n_row, height), jnp.float32),
        grid=(STEPS,),
        in_specs=[
            pl.BlockSpec(memory_space=pltpu.SMEM),
            pl.BlockSpec((1, height, depth), lambda s: (s, 0, 0)),
            pl.BlockSpec((n_row // STEPS, LIVE, TILE, TILE), lambda s: (s, 0, 0, 0)),
            pl.BlockSpec((height, width), lambda s: (0, 0)),
        ],
        out_specs=pl.BlockSpec((n_row, width // n_row, height), lambda s: (0, 0, 0)),
        scratch_shapes=[
            pltpu.VMEM((depth, width), jnp.bfloat16),
            pltpu.VMEM((height, width), jnp.float32),
        ],
        compiler_params=pltpu.CompilerParams(dimension_semantics=("arbitrary",), vmem_limit_bytes=56 * 1024 * 1024),
        name="product",
    )(tile_live, row_panel, col_panel, keep)


def scale_body(x_ref, out_ref):
    parts, _, height = x_ref.shape
    nodes = parts * height
    entries = x_ref[...]
    column_total = jnp.sum(jnp.sum(entries, axis=0), axis=1, keepdims=True)
    factor = nodes / column_total
    for p in range(parts):
        out_ref[0, :, p * height : (p + 1) * height] = entries[p] * factor


def scale(entries):
    parts, strips, height = entries.shape
    return pl.pallas_call(
        scale_body,
        out_shape=jax.ShapeDtypeStruct((1, strips, parts * height), jnp.float32),
        in_specs=[pl.BlockSpec(memory_space=pltpu.VMEM)],
        out_specs=pl.BlockSpec(memory_space=pltpu.VMEM),
        name="scale",
    )(entries)


def shards(transition, tile_live, prune_keep):
    units, plain = pack(tile_live, transition)
    col_panel = lax.all_gather(plain, "row", axis=0)
    row_panel = lax.all_gather(units, "col", axis=0)
    row_panel = spread(tile_live, row_panel, *transition.shape)
    strips = product(tile_live, row_panel, col_panel, prune_keep)
    entries = lax.all_to_all(strips, "row", split_axis=0, concat_axis=0, tiled=True)
    return scale(entries)


def solution(mesh):
    placed = (P("row", "col"), P(), P("row", "col"))
    return jax.shard_map(
        shards, mesh=mesh, in_specs=placed, out_specs=P("col", "row", None), check_vma=False
    )
```

time: 108 us -> 111 us (1.028)
  blocking collectives: 96.3 us -> 63.4 us
  waiting for transfers between devices: 0 us -> 17.6 us
  between operations: 0.02 us -> 13.4 us
  Pallas kernels: 11.8 us -> 16.3 us
    all_gather x2 -> x1, blocking collectives: 79.7 us -> 46.4 us  [shards(): row_panel = lax.all_gather(units, 'col', axis=0)]
    all_gather x0 -> x1, waiting for transfers between devices: none -> 17.6 us  [shards(): col_panel = lax.all_gather(plain, 'row', axis=0)]
    pallas_call x1 -> x2, Pallas kernels: 2.12 us -> 7.07 us  [the longest x1 5.07 us: spread(): pl.pallas_call(lambda *refs: spread_body(rows, cols, *refs), out_shape=ja...]
  transfers between devices with their start and end apart: 0 -> 1, of which waited for: 0 -> 1; matrix products, arithmetic and copies ran while one was open for 0% -> 0% of each run, Pallas kernels for 0% -> 5%
where the time goes in v4:
time: 111 us
  blocking collectives  63.4 us (57%)
  waiting for transfers between devices  17.6 us (16%)
  Pallas kernels  16.3 us (15%)
  between operations  13.4 us (12%)
    all_gather x1, blocking collectives, shards(): row_panel = lax.all_gather(units, 'col', axis=0)  46.4 us
    all_gather x1, waiting for transfers between devices, shards(): col_panel = lax.all_gather(plain, 'row', axis=0)  17.6 us
    all_to_all x1, blocking collectives, shards(): lax.all_to_all(strips, 'row', split_axis=0, concat_axis=0, tiled=True)  17 us
    pallas_call x1, Pallas kernels, product(): pl.pallas_call(lambda *refs: product_body(rows, cols, *refs), out_shape=j...  7.27 us
    pallas_call x1, Pallas kernels, spread(): pl.pallas_call(lambda *refs: spread_body(rows, cols, *refs), out_shape=ja...  5.07 us
  transfers between devices with their start and end apart: 1, of which 1 were waited for; matrix products, arithmetic and copies ran while one was open for 0% of the time, Pallas kernels for 5%

profile of v4, /device:TPU:1, one launch (start us, length us, event | category | flops | bytes accessed | tf_op | source)
XLA Modules:
  0.0 110.7 jit_solution(9453208092319974303)
XLA Ops:
  6.5 0.0 all-gather.5.cloned.1.call-start
  6.5 2.0 %pack.1 = (s16[4,128,128]{2,1,0:T(8,128)(2,1)}, bf16[4,128,128]{2,1,0:T(8,128)(2,1)}) custom-call(s32[64,64]{1,0:T(8,128)} %refs_0_.3, bf16[256,512]{1,0:T(8,128)(2,1)} %x_ref.1), custom_call_target="tpu_custom_call" | custom-call | tf_op jit(solution)/shard_map/pack/pallas_call | solution.py:37
  8.5 0.0 all-gather.5.cloned.1.call-update
  8.6 46.4 %all-gather.6 = s16[64,128,128]{2,1,0:T(8,128)(2,1)} all-gather(s16[4,128,128]{2,1,0:T(8,128)(2,1)} %get-tuple-element.7), channel_id=2, replica_groups=mesh['row'=32,'col'=16] {'col'}, dimensions={0}, use_global_device_ids=true | all-gather | bytes 2228224 | tf_op jit(solution)/shard_map/all_gather | solution.py:154
  55.0 5.1 %spread.1.refs_1_ = bf16[4,256,2048]{2,1,0:T(8,128)(2,1)} custom-call(s32[64,64]{1,0:T(8,128)} %refs_0_.3, s16[16,4,128,128]{3,2,1,0:T(8,128)(2,1)} %bitcast.2), custom_call_target="tpu_custom_call" | custom-call | bytes 6291456 | tf_op jit(solution)/shard_map/spread/pallas_call | solution.py:69
  60.1 17.6 %all-gather.5.cloned.1.call-done = bf16[128,128,128]{2,1,0:T(8,128)(2,1)} async-done(((bf16[4,128,128]{2,1,0:T(8,128)(2,1)}), bf16[128,128,128]{2,1,0:T(8,128)(2,1)}) %all-gather.5.cloned.1.call-update) | async-done | bytes 4194320 | tf_op jit(solution)/shard_map/all_gather | solution.py:153
  77.6 7.3 %product.1 = f32[32,16,256]{2,1,0:T(8,128)} custom-call(s32[64,64]{1,0:T(8,128)} %refs_0_.3, bf16[4,256,2048]{2,1,0:T(8,128)(2,1)} %spread.1.refs_1_, bf16[32,4,128,128]{3,2,1,0:T(8,128)(2,1)} %bitcast.3, s32[256,512]{1,0:T(8,128)} %refs_3_.1), custom_call_target="tpu_custom_call" | custom-call | tf_op jit(solution)/shard_map/product/pallas_call | solution.py:110
  84.9 17.0 %all_to_all.5.x_ref = f32[32,16,256]{2,1,0:T(8,128)} all-to-all(f32[32,16,256]{2,1,0:T(8,128)} %product.1), channel_id=1, replica_groups=mesh['row'=32,'col'=16] {'row'}, dimensions={0} | all-to-all | bytes 1048576 | tf_op jit(solution)/shard_map/all_to_all | solution.py:157
  101.9 2.0 %scale.1 = f32[1,16,8192]{2,1,0:T(8,128)} custom-call(f32[32,16,256]{2,1,0:T(8,128)} %all_to_all.5.x_ref), custom_call_target="tpu_custom_call" | custom-call | tf_op jit(solution)/shard_map/scale/pallas_call | solution.py:142
Async XLA Ops:
  6.5 71.1 %all-gather.5.cloned.1.call-start = ((), (), s32[]{:S(2)}) async-start(), calls=%async_computation.1 | async-start | bytes 4325376 | tf_op jit(solution)/shard_map/all_gather | solution.py:153
Sparse Core Ops, SparseCore 0:
  10.5 67.0 all-gather.4

commit v5 on v1

v5 whole, which is shorter than its diff:
```python
import jax
import jax.numpy as jnp
from jax import lax
from jax.experimental import pallas as pl
from jax.experimental.pallas import tpu as pltpu
from jax.sharding import PartitionSpec as P

TILE = 128
LIVE = 4
UNIT = 16384.0
PARTS = 2


def spots(rows, cols):
    return [(a, b, slice(a * TILE, (a + 1) * TILE), slice(b * TILE, (b + 1) * TILE)) for a in range(rows) for b in range(cols)]


def pack_body(live, x_ref, out_ref):
    rows, cols = x_ref.shape[0] // TILE, x_ref.shape[1] // TILE
    top, left = lax.axis_index("row") * rows, lax.axis_index("col") * cols
    slot = jnp.int32(0)
    for a, b, across, down in spots(rows, cols):
        flag = live[top + a, left + b]

        @pl.when((flag > 0) & (slot < LIVE))
        def _(slot=slot, across=across, down=down):
            units = x_ref[across, down].astype(jnp.float32).T * UNIT
            out_ref[slot] = units.astype(jnp.int32).astype(jnp.int16)

        slot = slot + flag


def pack(tile_live, transition):
    return pl.pallas_call(
        pack_body,
        out_shape=jax.ShapeDtypeStruct((LIVE, TILE, TILE), jnp.int16),
        in_specs=[pl.BlockSpec(memory_space=pltpu.SMEM), pl.BlockSpec(memory_space=pltpu.VMEM)],
        out_specs=pl.BlockSpec(memory_space=pltpu.VMEM),
        name="pack",
    )(tile_live, transition)


def placing(live, top, left, rows, cols, slots_ref, dense_ref, down, across):
    slot, tasks = jnp.int32(0), []
    for spot, (a, b, _, _) in enumerate(spots(rows, cols)):
        flag = live[top + a, left + b]

        def place(flag=flag, slot=slot if spot < LIVE else jnp.minimum(slot, LIVE - 1), a=a, b=b):
            tile = slots_ref[slot].astype(jnp.float32)
            tile = jnp.where(flag > 0, tile, 0.0).astype(jnp.bfloat16)
            dense_ref[down + b * TILE : down + (b + 1) * TILE, across + a * TILE : across + (a + 1) * TILE] = tile

        tasks.append(place)
        slot = slot + flag
    return tasks


def product_body(rows, cols, live, a_ref, b_ref, keep_ref, out_ref, a_dense, b_dense, total):
    panels = a_ref.shape[0]
    each = b_ref.shape[0] // panels
    top, left = lax.axis_index("row") * rows, lax.axis_index("col") * cols

    def tasks_of(panel):
        a_to, b_to = a_dense.at[panel % 2], b_dense.at[panel % 2]
        tasks = placing(live, top, panel * cols, rows, cols, a_ref.at[panel], a_to, 0, 0)
        for e in range(each):
            group = panel * each + e
            tasks += placing(live, group * rows, left, rows, cols, b_ref.at[group], b_to, 0, e * rows * TILE)
        return tasks

    keep = keep_ref[...].astype(jnp.float32).T * (1.0 / (UNIT * UNIT))
    for place in tasks_of(0):
        place()
    for panel in range(panels):
        later = tasks_of(panel + 1) if panel + 1 < panels else []
        share, high = len(later) // PARTS, total.shape[0] // PARTS
        for part in range(PARTS):
            lines = slice(part * high, (part + 1) * high)
            product = jnp.dot(
                b_dense[panel % 2, lines, :], a_dense[panel % 2], preferred_element_type=jnp.float32
            )
            total[lines, :] = product if panel == 0 else total[lines, :] + product
            for place in later[part * share : (part + 1) * share]:
                place()
    kept = total[...] * keep
    out_ref[...] = (kept * kept).reshape(out_ref.shape)


def product(tile_live, row_panel, col_panel, keep):
    n_row = col_panel.shape[0]
    height, width = keep.shape
    rows, cols = height // TILE, width // TILE
    in_vmem = pl.BlockSpec(memory_space=pltpu.VMEM)
    return pl.pallas_call(
        lambda *refs: product_body(rows, cols, *refs),
        out_shape=jax.ShapeDtypeStruct((n_row, width // n_row, height), jnp.float32),
        in_specs=[pl.BlockSpec(memory_space=pltpu.SMEM), in_vmem, in_vmem, in_vmem],
        out_specs=in_vmem,
        scratch_shapes=[
            pltpu.VMEM((2, width, height), jnp.bfloat16),
            pltpu.VMEM((2, width, width), jnp.bfloat16),
            pltpu.VMEM((width, height), jnp.float32),
        ],
        compiler_params=pltpu.CompilerParams(vmem_limit_bytes=32 * 1024 * 1024),
        name="product",
    )(tile_live, row_panel, col_panel, keep)


def scale_body(x_ref, out_ref):
    parts, _, height = x_ref.shape
    nodes = parts * height
    entries = x_ref[...]
    column_total = jnp.sum(jnp.sum(entries, axis=0), axis=1, keepdims=True)
    factor = nodes / column_total
    for p in range(parts):
        out_ref[0, :, p * height : (p + 1) * height] = entries[p] * factor


def scale(entries):
    parts, strips, height = entries.shape
    return pl.pallas_call(
        scale_body,
        out_shape=jax.ShapeDtypeStruct((1, strips, parts * height), jnp.float32),
        in_specs=[pl.BlockSpec(memory_space=pltpu.VMEM)],
        out_specs=pl.BlockSpec(memory_space=pltpu.VMEM),
        name="scale",
    )(entries)


def shards(transition, tile_live, prune_keep):
    packed = pack(tile_live, transition)
    row_panel = lax.all_gather(packed, "col", axis=0)
    col_panel = lax.all_gather(packed, "row", axis=0)
    strips = product(tile_live, row_panel, col_panel, prune_keep)
    entries = lax.all_to_all(strips, "row", split_axis=0, concat_axis=0, tiled=True)
    return scale(entries)


def solution(mesh):
    placed = (P("row", "col"), P(), P("row", "col"))
    return jax.shard_map(
        shards, mesh=mesh, in_specs=placed, out_specs=P("col", "row", None), check_vma=False
    )
```

time: 108 us -> 107 us (level)
  Pallas kernels: 11.8 us -> 10.3 us
    pallas_call x1, Pallas kernels: 7.67 us -> 5.91 us  [product(): pl.pallas_call(lambda *refs: product_body(rows, cols, *refs), out_shape=j...]
    all_gather x1, blocking collectives: 34.9 us -> 36.4 us  [shards(): col_panel = lax.all_gather(packed, 'row', axis=0)]
where the time goes in v5:
time: 107 us
  blocking collectives  96.7 us (90%)
  Pallas kernels  10.3 us (10%)
    all_gather x1, blocking collectives, shards(): row_panel = lax.all_gather(packed, 'col', axis=0)  44 us
    all_gather x1, blocking collectives, shards(): col_panel = lax.all_gather(packed, 'row', axis=0)  36.4 us
    all_to_all x1, blocking collectives, shards(): lax.all_to_all(strips, 'row', split_axis=0, concat_axis=0, tiled=True)  16.4 us
    pallas_call x1, Pallas kernels, product(): pl.pallas_call(lambda *refs: product_body(rows, cols, *refs), out_shape=j...  5.91 us
    pallas_call x1, Pallas kernels, pack(): pl.pallas_call(pack_body, out_shape=jax.ShapeDtypeStruct((LIVE, TILE, TIL...  2.36 us

profile of v5, /device:TPU:1, one launch (start us, length us, event | category | flops | bytes accessed | tf_op | source)
XLA Modules:
  0.0 107.0 jit_solution(4863323487925209864)
XLA Ops:
  0.0 0.0 copy-start.1
  0.0 0.0 copy-start
  0.0 2.4 %pack.1 = s16[4,128,128]{2,1,0:T(8,128)(2,1)} custom-call(s32[64,64]{1,0:T(8,128)} %refs_0_.1, bf16[256,512]{1,0:T(8,128)(2,1)} %x_ref.1), custom_call_target="tpu_custom_call" | custom-call | tf_op jit(solution)/shard_map/pack/pallas_call | solution.py:34
  2.4 44.0 %all-gather.4 = s16[64,128,128]{2,1,0:T(8,128)(2,1)S(1)} all-gather(s16[4,128,128]{2,1,0:T(8,128)(2,1)} %pack.1), channel_id=2, replica_groups=mesh['row'=32,'col'=16] {'col'}, dimensions={0}, use_global_device_ids=true | all-gather | bytes 2228224 | tf_op jit(solution)/shard_map/all_gather | solution.py:132
  46.3 36.4 %all-gather.5 = s16[128,128,128]{2,1,0:T(8,128)(2,1)S(1)} all-gather(s16[4,128,128]{2,1,0:T(8,128)(2,1)} %pack.1), channel_id=3, replica_groups=mesh['row'=32,'col'=16] {'row'}, dimensions={0}, use_global_device_ids=true | all-gather | bytes 4325376 | tf_op jit(solution)/shard_map/all_gather | solution.py:133
  82.7 0.0 copy-done.1
  82.7 0.0 copy-done
  82.7 5.9 %product.1 = f32[32,16,256]{2,1,0:T(8,128)S(1)} custom-call(s32[64,64]{1,0:T(8,128)S(1)} %copy-done.1, s16[16,4,128,128]{3,2,1,0:T(8,128)(2,1)S(1)} %bitcast.3, s16[32,4,128,128]{3,2,1,0:T(8,128)(2,1)S(1)} %bitcast.2, s32[256,512]{1,0:T(8,128)S(1)} %copy-done), custom_call_target="tpu_custom_call" | custom-call | tf_op jit(solution)/shard_map/product/pallas_call | solution.py:94
  88.6 16.4 %all_to_all.5.x_ref = f32[32,16,256]{2,1,0:T(8,128)} all-to-all(f32[32,16,256]{2,1,0:T(8,128)S(1)} %product.1), channel_id=1, replica_groups=mesh['row'=32,'col'=16] {'row'}, dimensions={0} | all-to-all | bytes 1048576 | tf_op jit(solution)/shard_map/all_to_all | solution.py:135
  105.0 2.0 %scale.1 = f32[1,16,8192]{2,1,0:T(8,128)} custom-call(f32[32,16,256]{2,1,0:T(8,128)} %all_to_all.5.x_ref), custom_call_target="tpu_custom_call" | custom-call | tf_op jit(solution)/shard_map/scale/pallas_call | solution.py:121
Async XLA Ops:
  0.0 82.7 %copy-start.1 = (s32[64,64]{1,0:T(8,128)S(1)}, s32[64,64]{1,0:T(8,128)}, u32[]{:S(2)}) copy-start(s32[64,64]{1,0:T(8,128)} %refs_0_.1) | copy-start | bytes 49156
  0.0 82.7 %copy-start = (s32[256,512]{1,0:T(8,128)S(1)}, s32[256,512]{1,0:T(8,128)}, u32[]{:S(2)}) copy-start(s32[256,512]{1,0:T(8,128)} %refs_3_.1) | copy-start | bytes 1572868

commit v6 on v5

--- a/solution.py
+++ b/solution.py
@@ -9,15 +9,24 @@
 LIVE = 4
 UNIT = 16384.0
 PARTS = 2
+GROUP = 8
 
 
 def spots(rows, cols):
     return [(a, b, slice(a * TILE, (a + 1) * TILE), slice(b * TILE, (b + 1) * TILE)) for a in range(rows) for b in range(cols)]
 
 
-def pack_body(live, x_ref, out_ref):
+def pack_body(live_hbm, x_hbm, out_ref, live, x_ref, arrived):
     rows, cols = x_ref.shape[0] // TILE, x_ref.shape[1] // TILE
     top, left = lax.axis_index("row") * rows, lax.axis_index("col") * cols
+    group = pl.multiple_of(top // GROUP * GROUP, GROUP)
+    flags_in = pltpu.make_async_copy(live_hbm.at[pl.ds(group, GROUP)], live, arrived.at[0])
+    block_in = pltpu.make_async_copy(x_hbm, x_ref, arrived.at[1])
+    flags_in.start()
+    block_in.start()
+    flags_in.wait()
+    block_in.wait()
+    top = top - group
     slot = jnp.int32(0)
     for a, b, across, down in spots(rows, cols):
         flag = live[top + a, left + b]
@@ -34,8 +43,13 @@
     return pl.pallas_call(
         pack_body,
         out_shape=jax.ShapeDtypeStruct((LIVE, TILE, TILE), jnp.int16),
-        in_specs=[pl.BlockSpec(memory_space=pltpu.SMEM), pl.BlockSpec(memory_space=pltpu.VMEM)],
+        in_specs=[pl.BlockSpec(memory_space=pl.ANY)] * 2,
         out_specs=pl.BlockSpec(memory_space=pltpu.VMEM),
+        scratch_shapes=[
+            pltpu.SMEM((GROUP, tile_live.shape[1]), tile_live.dtype),
+            pltpu.VMEM(transition.shape, transition.dtype),
+            pltpu.SemaphoreType.DMA((2,)),
+        ],
         name="pack",
     )(tile_live, transition)
 
@@ -55,7 +69,9 @@
     return tasks
 
 
-def product_body(rows, cols, live, a_ref, b_ref, keep_ref, out_ref, a_dense, b_dense, total):
+def product_body(rows, cols, live_hbm, a_ref, b_ref, keep_ref, out_ref, live, a_dense, b_dense, total, arrived):
+    flags_in = pltpu.make_async_copy(live_hbm, live, arrived)
+    flags_in.start()
     panels = a_ref.shape[0]
     each = b_ref.shape[0] // panels
     top, left = lax.axis_index("row") * rows, lax.axis_index("col") * cols
@@ -69,6 +85,7 @@
         return tasks
 
     keep = keep_ref[...].astype(jnp.float32).T * (1.0 / (UNIT * UNIT))
+    flags_in.wait()
     for place in tasks_of(0):
         place()
     for panel in range(panels):
@@ -94,12 +111,14 @@
     return pl.pallas_call(
         lambda *refs: product_body(rows, cols, *refs),
         out_shape=jax.ShapeDtypeStruct((n_row, width // n_row, height), jnp.float32),
-        in_specs=[pl.BlockSpec(memory_space=pltpu.SMEM), in_vmem, in_vmem, in_vmem],
+        in_specs=[pl.BlockSpec(memory_space=pl.ANY), in_vmem, in_vmem, in_vmem],
         out_specs=in_vmem,
         scratch_shapes=[
+            pltpu.SMEM(tile_live.shape, tile_live.dtype),
             pltpu.VMEM((2, width, height), jnp.bfloat16),
             pltpu.VMEM((2, width, width), jnp.bfloat16),
             pltpu.VMEM((width, height), jnp.float32),
+            pltpu.SemaphoreType.DMA,
         ],
         compiler_params=pltpu.CompilerParams(vmem_limit_bytes=32 * 1024 * 1024),
         name="product",
@@ -123,6 +142,7 @@
         out_shape=jax.ShapeDtypeStruct((1, strips, parts * height), jnp.float32),
         in_specs=[pl.BlockSpec(memory_space=pltpu.VMEM)],
         out_specs=pl.BlockSpec(memory_space=pltpu.VMEM),
+        compiler_params=pltpu.CompilerParams(vmem_limit_bytes=4 * 1024 * 1024),
         name="scale",
     )(entries)
 

time: 107 us -> 105 us (0.981)
  Pallas kernels: 10.3 us -> 8.81 us
    all_gather x1, blocking collectives: 36.4 us -> 34.8 us  [shards(): col_panel = lax.all_gather(packed, 'row', axis=0)]
    all_gather x1, blocking collectives: 44 us -> 45.1 us  [shards(): row_panel = lax.all_gather(packed, 'col', axis=0)]
where the time goes in v6:
time: 105 us
  blocking collectives  96.4 us (92%)
  Pallas kernels  8.81 us (8%)
    all_gather x1, blocking collectives, shards(): row_panel = lax.all_gather(packed, 'col', axis=0)  45.1 us
    all_gather x1, blocking collectives, shards(): col_panel = lax.all_gather(packed, 'row', axis=0)  34.8 us
    all_to_all x1, blocking collectives, shards(): lax.all_to_all(strips, 'row', split_axis=0, concat_axis=0, tiled=True)  16.5 us
    pallas_call x1, Pallas kernels, product(): pl.pallas_call(lambda *refs: product_body(rows, cols, *refs), out_shape=j...  5.93 us

profile of v6, /device:TPU:1, one launch (start us, length us, event | category | flops | bytes accessed | tf_op | source)
XLA Modules:
  0.0 105.2 jit_solution(3850477791947969411)
XLA Ops:
  0.0 0.0 copy-start.1
  0.0 0.0 copy-start
  0.0 1.9 %pack.1 = s16[4,128,128]{2,1,0:T(8,128)(2,1)} custom-call(s32[64,64]{1,0:T(8,128)} %refs_0_.1, bf16[256,512]{1,0:T(8,128)(2,1)} %x_hbm.1), custom_call_target="tpu_custom_call" | custom-call | tf_op jit(solution)/shard_map/pack/pallas_call | solution.py:43
  1.9 45.1 %all-gather.4 = s16[64,128,128]{2,1,0:T(8,128)(2,1)S(1)} all-gather(s16[4,128,128]{2,1,0:T(8,128)(2,1)} %pack.1), channel_id=2, replica_groups=mesh['row'=32,'col'=16] {'col'}, dimensions={0}, use_global_device_ids=true | all-gather | bytes 2228224 | tf_op jit(solution)/shard_map/all_gather | solution.py:152
  47.0 34.8 %all-gather.5 = s16[128,128,128]{2,1,0:T(8,128)(2,1)S(1)} all-gather(s16[4,128,128]{2,1,0:T(8,128)(2,1)} %pack.1), channel_id=3, replica_groups=mesh['row'=32,'col'=16] {'row'}, dimensions={0}, use_global_device_ids=true | all-gather | bytes 4325376 | tf_op jit(solution)/shard_map/all_gather | solution.py:153
  81.8 0.0 copy-done.1
  81.8 0.0 copy-done
  81.8 5.9 %product.1 = f32[32,16,256]{2,1,0:T(8,128)S(1)} custom-call(s32[64,64]{1,0:T(8,128)S(1)} %copy-done.1, s16[16,4,128,128]{3,2,1,0:T(8,128)(2,1)S(1)} %bitcast.3, s16[32,4,128,128]{3,2,1,0:T(8,128)(2,1)S(1)} %bitcast.2, s32[256,512]{1,0:T(8,128)S(1)} %copy-done), custom_call_target="tpu_custom_call" | custom-call | tf_op jit(solution)/shard_map/product/pallas_call | solution.py:111
  87.8 16.5 %all_to_all.5.x_ref = f32[32,16,256]{2,1,0:T(8,128)S(1)} all-to-all(f32[32,16,256]{2,1,0:T(8,128)S(1)} %product.1), channel_id=1, replica_groups=mesh['row'=32,'col'=16] {'row'}, dimensions={0} | all-to-all | bytes 1048576 | tf_op jit(solution)/shard_map/all_to_all | solution.py:155
  104.3 0.9 scale.1
Async XLA Ops:
  0.0 81.8 %copy-start.1 = (s32[64,64]{1,0:T(8,128)S(1)}, s32[64,64]{1,0:T(8,128)}, u32[]{:S(2)}) copy-start(s32[64,64]{1,0:T(8,128)} %refs_0_.1) | copy-start | bytes 49156
  0.0 81.8 %copy-start = (s32[256,512]{1,0:T(8,128)S(1)}, s32[256,512]{1,0:T(8,128)}, u32[]{:S(2)}) copy-start(s32[256,512]{1,0:T(8,128)} %refs_3_.1) | copy-start | bytes 1572868

commit v7 on v6

--- a/solution.py
+++ b/solution.py
@@ -43,13 +43,14 @@
     return pl.pallas_call(
         pack_body,
         out_shape=jax.ShapeDtypeStruct((LIVE, TILE, TILE), jnp.int16),
-        in_specs=[pl.BlockSpec(memory_space=pl.ANY)] * 2,
+        in_specs=[pl.BlockSpec(memory_space=pltpu.HBM)] * 2,
         out_specs=pl.BlockSpec(memory_space=pltpu.VMEM),
         scratch_shapes=[
             pltpu.SMEM((GROUP, tile_live.shape[1]), tile_live.dtype),
             pltpu.VMEM(transition.shape, transition.dtype),
             pltpu.SemaphoreType.DMA((2,)),
         ],
+        compiler_params=pltpu.CompilerParams(vmem_limit_bytes=4 * 1024 * 1024),
         name="pack",
     )(tile_live, transition)
 

time: 105 us -> 106 us (level)
  local copies, waits for them, and re-layouts: 0.01 us -> 1.71 us
    unnamed x4 -> x8, local copies, waits for them, and re-layouts: 0.01 us -> 1.71 us
where the time goes in v7:
time: 106 us
  blocking collectives  96.4 us (91%)
  Pallas kernels  7.77 us (7%)
  local copies, waits for them, and re-layouts  1.71 us (2%)
    all_gather x1, blocking collectives, shards(): row_panel = lax.all_gather(packed, 'col', axis=0)  44.3 us
    all_gather x1, blocking collectives, shards(): col_panel = lax.all_gather(packed, 'row', axis=0)  35.6 us
    all_to_all x1, blocking collectives, shards(): lax.all_to_all(strips, 'row', split_axis=0, concat_axis=0, tiled=True)  16.6 us
    pallas_call x1, Pallas kernels, product(): pl.pallas_call(lambda *refs: product_body(rows, cols, *refs), out_shape=j...  5.93 us

profile of v7, /device:TPU:1, one launch (start us, length us, event | category | flops | bytes accessed | tf_op | source)
XLA Modules:
  0.0 106.0 jit_solution(3744355182189968640)
XLA Ops:
  0.0 0.0 copy-start.1
  0.0 0.9 copy-done.1
  1.0 0.0 copy-start.2
  1.0 0.8 copy-done.2
  1.7 0.0 copy-start
  1.7 0.0 copy-start.3
  1.7 0.9 pack.1
  2.6 44.3 %all-gather.4 = s16[64,128,128]{2,1,0:T(8,128)(2,1)S(1)} all-gather(s16[4,128,128]{2,1,0:T(8,128)(2,1)S(1)} %pack.1), channel_id=2, replica_groups=mesh['row'=32,'col'=16] {'col'}, dimensions={0}, use_global_device_ids=true | all-gather | bytes 2228224 | tf_op jit(solution)/shard_map/all_gather | solution.py:153
  46.9 35.6 %all-gather.5 = s16[128,128,128]{2,1,0:T(8,128)(2,1)S(1)} all-gather(s16[4,128,128]{2,1,0:T(8,128)(2,1)S(1)} %pack.1), channel_id=3, replica_groups=mesh['row'=32,'col'=16] {'row'}, dimensions={0}, use_global_device_ids=true | all-gather | bytes 4325376 | tf_op jit(solution)/shard_map/all_gather | solution.py:154
  82.5 0.0 copy-done
  82.5 0.0 copy-done.3
  82.5 5.9 %product.1 = f32[32,16,256]{2,1,0:T(8,128)S(1)} custom-call(s32[64,64]{1,0:T(8,128)S(1)} %copy-done.3, s16[16,4,128,128]{3,2,1,0:T(8,128)(2,1)S(1)} %bitcast.3, s16[32,4,128,128]{3,2,1,0:T(8,128)(2,1)S(1)} %bitcast.2, s32[256,512]{1,0:T(8,128)S(1)} %copy-done), custom_call_target="tpu_custom_call" | custom-call | tf_op jit(solution)/shard_map/product/pallas_call | solution.py:112
  88.4 16.6 %all_to_all.5.x_ref = f32[32,16,256]{2,1,0:T(8,128)S(1)} all-to-all(f32[32,16,256]{2,1,0:T(8,128)S(1)} %product.1), channel_id=1, replica_groups=mesh['row'=32,'col'=16] {'row'}, dimensions={0} | all-to-all | bytes 1048576 | tf_op jit(solution)/shard_map/all_to_all | solution.py:156
  105.0 0.9 scale.1
Async XLA Ops:
  0.0 0.9 copy-start.1
  1.0 0.8 copy-start.2
  1.7 80.8 %copy-start = (s32[256,512]{1,0:T(8,128)S(1)}, s32[256,512]{1,0:T(8,128)}, u32[]{:S(2)}) copy-start(s32[256,512]{1,0:T(8,128)} %refs_3_.1) | copy-start | bytes 1572868
  1.7 80.8 %copy-start.3 = (s32[64,64]{1,0:T(8,128)S(1)}, s32[64,64]{1,0:T(8,128)}, u32[]{:S(2)}) copy-start(s32[64,64]{1,0:T(8,128)} %refs_0_.1) | copy-start | bytes 49156

commit v8 on v6

--- a/solution.py
+++ b/solution.py
@@ -8,6 +8,9 @@
 TILE = 128
 LIVE = 4
 UNIT = 16384.0
+LEVELS = 32700.0
+OCTAVE = 0.6931471805599453 / 1024
+SMALLEST = 2.0**-20
 PARTS = 2
 GROUP = 8
 
@@ -100,7 +103,13 @@
             for place in later[part * share : (part + 1) * share]:
                 place()
     kept = total[...] * keep
-    out_ref[...] = (kept * kept).reshape(out_ref.shape)
+    strips, height = out_ref.shape[:2], total.shape[1]
+    largest = jnp.maximum(jnp.max(kept, axis=1, keepdims=True), SMALLEST)
+    code = jnp.ceil(jnp.log(largest) * (1.0 / OCTAVE))
+    levels = (kept * (LEVELS / jnp.exp(code * OCTAVE)) + 0.5).astype(jnp.int32).astype(jnp.int16)
+    out_ref[:, :, :height] = levels.reshape(*strips, height)
+    code = jnp.broadcast_to(code, (code.shape[0], TILE)).astype(jnp.int32).astype(jnp.int16)
+    out_ref[:, :, height:] = code.reshape(*strips, TILE)
 
 
 def product(tile_live, row_panel, col_panel, keep):
@@ -110,7 +119,7 @@
     in_vmem = pl.BlockSpec(memory_space=pltpu.VMEM)
     return pl.pallas_call(
         lambda *refs: product_body(rows, cols, *refs),
-        out_shape=jax.ShapeDtypeStruct((n_row, width // n_row, height), jnp.float32),
+        out_shape=jax.ShapeDtypeStruct((n_row, width // n_row, height + TILE), jnp.int16),
         in_specs=[pl.BlockSpec(memory_space=pl.ANY), in_vmem, in_vmem, in_vmem],
         out_specs=in_vmem,
         scratch_shapes=[
@@ -126,9 +135,12 @@
 
 
 def scale_body(x_ref, out_ref):
-    parts, _, height = x_ref.shape
+    parts, strips, height = x_ref.shape
+    height = height - TILE
     nodes = parts * height
-    entries = x_ref[...]
+    unit = jnp.exp(x_ref[:, :, height:].astype(jnp.float32) * OCTAVE) * (1.0 / LEVELS)
+    kept = [x_ref[:, :, at : at + TILE].astype(jnp.float32) * unit for at in range(0, height, TILE)]
+    entries = jnp.concatenate([part * part for part in kept], axis=2)
     column_total = jnp.sum(jnp.sum(entries, axis=0), axis=1, keepdims=True)
     factor = nodes / column_total
     for p in range(parts):
@@ -137,6 +149,7 @@
 
 def scale(entries):
     parts, strips, height = entries.shape
+    height = height - TILE
     return pl.pallas_call(
         scale_body,
         out_shape=jax.ShapeDtypeStruct((1, strips, parts * height), jnp.float32),

time: 105 us -> 104 us (level)
  blocking collectives: 96.4 us -> 94.8 us
    all_to_all x1, blocking collectives: 16.5 us -> 15.2 us  [shards(): lax.all_to_all(strips, 'row', split_axis=0, concat_axis=0, tiled=True)]
where the time goes in v8:
time: 104 us
  blocking collectives  94.8 us (91%)
  Pallas kernels  9.32 us (9%)
    all_gather x1, blocking collectives, shards(): row_panel = lax.all_gather(packed, 'col', axis=0)  44.7 us
    all_gather x1, blocking collectives, shards(): col_panel = lax.all_gather(packed, 'row', axis=0)  34.9 us
    all_to_all x1, blocking collectives, shards(): lax.all_to_all(strips, 'row', split_axis=0, concat_axis=0, tiled=True)  15.2 us
    pallas_call x1, Pallas kernels, product(): pl.pallas_call(lambda *refs: product_body(rows, cols, *refs), out_shape=j...  6.16 us
    pallas_call x1, Pallas kernels, pack(): pl.pallas_call(pack_body, out_shape=jax.ShapeDtypeStruct((LIVE, TILE, TIL...  2.12 us

profile of v8, /device:TPU:1, one launch (start us, length us, event | category | flops | bytes accessed | tf_op | source)
XLA Modules:
  0.0 104.2 jit_solution(8964035554803074217)
XLA Ops:
  0.0 0.0 copy-start.1
  0.0 0.0 copy-start
  0.0 2.1 %pack.1 = s16[4,128,128]{2,1,0:T(8,128)(2,1)} custom-call(s32[64,64]{1,0:T(8,128)} %refs_0_.1, bf16[256,512]{1,0:T(8,128)(2,1)} %x_hbm.1), custom_call_target="tpu_custom_call" | custom-call | tf_op jit(solution)/shard_map/pack/pallas_call | solution.py:46
  2.1 44.7 %all-gather.4 = s16[64,128,128]{2,1,0:T(8,128)(2,1)S(1)} all-gather(s16[4,128,128]{2,1,0:T(8,128)(2,1)} %pack.1), channel_id=2, replica_groups=mesh['row'=32,'col'=16] {'col'}, dimensions={0}, use_global_device_ids=true | all-gather | bytes 2228224 | tf_op jit(solution)/shard_map/all_gather | solution.py:165
  46.9 34.9 %all-gather.5 = s16[128,128,128]{2,1,0:T(8,128)(2,1)S(1)} all-gather(s16[4,128,128]{2,1,0:T(8,128)(2,1)} %pack.1), channel_id=3, replica_groups=mesh['row'=32,'col'=16] {'row'}, dimensions={0}, use_global_device_ids=true | all-gather | bytes 4325376 | tf_op jit(solution)/shard_map/all_gather | solution.py:166
  81.8 0.0 copy-done.1
  81.8 0.0 copy-done
  81.8 6.2 %product.1 = s16[32,16,384]{2,1,0:T(8,128)(2,1)S(1)} custom-call(s32[64,64]{1,0:T(8,128)S(1)} %copy-done.1, s16[16,4,128,128]{3,2,1,0:T(8,128)(2,1)S(1)} %bitcast.3, s16[32,4,128,128]{3,2,1,0:T(8,128)(2,1)S(1)} %bitcast.2, s32[256,512]{1,0:T(8,128)S(1)} %copy-done), custom_call_target="tpu_custom_call" | custom-call | tf_op jit(solution)/shard_map/product/pallas_call | solution.py:120
  88.0 15.2 %all_to_all.5.x_ref = s16[32,16,384]{2,1,0:T(8,128)(2,1)S(1)} all-to-all(s16[32,16,384]{2,1,0:T(8,128)(2,1)S(1)} %product.1), channel_id=1, replica_groups=mesh['row'=32,'col'=16] {'row'}, dimensions={0} | all-to-all | bytes 786432 | tf_op jit(solution)/shard_map/all_to_all | solution.py:168
  103.2 1.0 %scale.1 = f32[1,16,8192]{2,1,0:T(8,128)} custom-call(s16[32,16,384]{2,1,0:T(8,128)(2,1)S(1)} %all_to_all.5.x_ref), custom_call_target="tpu_custom_call" | custom-call | tf_op jit(solution)/shard_map/scale/pallas_call | solution.py:153
Async XLA Ops:
  0.0 81.8 %copy-start.1 = (s32[64,64]{1,0:T(8,128)S(1)}, s32[64,64]{1,0:T(8,128)}, u32[]{:S(2)}) copy-start(s32[64,64]{1,0:T(8,128)} %refs_0_.1) | copy-start | bytes 49156
  0.0 81.8 %copy-start = (s32[256,512]{1,0:T(8,128)S(1)}, s32[256,512]{1,0:T(8,128)}, u32[]{:S(2)}) copy-start(s32[256,512]{1,0:T(8,128)} %refs_3_.1) | copy-start | bytes 1572868

commit v9 on v8

--- a/solution.py
+++ b/solution.py
@@ -162,8 +162,9 @@
 
 def shards(transition, tile_live, prune_keep):
     packed = pack(tile_live, transition)
+    col_panel = lax.all_gather(packed, "row", axis=0)
+    packed, col_panel = lax.optimization_barrier((packed, col_panel))
     row_panel = lax.all_gather(packed, "col", axis=0)
-    col_panel = lax.all_gather(packed, "row", axis=0)
     strips = product(tile_live, row_panel, col_panel, prune_keep)
     entries = lax.all_to_all(strips, "row", split_axis=0, concat_axis=0, tiled=True)
     return scale(entries)

time: 104 us -> 105 us (level)
    all_to_all x1, blocking collectives: 15.2 us -> 21.2 us  [shards(): lax.all_to_all(strips, 'row', split_axis=0, concat_axis=0, tiled=True)]
    all_gather x1, blocking collectives: 44.7 us -> 41.3 us  [shards(): row_panel = lax.all_gather(packed, 'col', axis=0)]
    all_gather x1, blocking collectives: 34.9 us -> 33.1 us  [shards(): col_panel = lax.all_gather(packed, 'row', axis=0)]
where the time goes in v9:
time: 105 us
  blocking collectives  95.7 us (91%)
  Pallas kernels  9.13 us (9%)
    all_gather x1, blocking collectives, shards(): row_panel = lax.all_gather(packed, 'col', axis=0)  41.3 us
    all_gather x1, blocking collectives, shards(): col_panel = lax.all_gather(packed, 'row', axis=0)  33.1 us
    all_to_all x1, blocking collectives, shards(): lax.all_to_all(strips, 'row', split_axis=0, concat_axis=0, tiled=True)  21.2 us
    pallas_call x1, Pallas kernels, product(): pl.pallas_call(lambda *refs: product_body(rows, cols, *refs), out_shape=j...  6.16 us

profile of v9, /device:TPU:1, one launch (start us, length us, event | category | flops | bytes accessed | tf_op | source)
XLA Modules:
  0.0 104.8 jit_solution(1122067554030952774)
XLA Ops:
  0.0 0.0 copy-start.1
  0.0 0.0 copy-start
  0.0 1.9 %pack.1 = s16[4,128,128]{2,1,0:T(8,128)(2,1)} custom-call(s32[64,64]{1,0:T(8,128)} %refs_0_.1, bf16[256,512]{1,0:T(8,128)(2,1)} %x_hbm.1), custom_call_target="tpu_custom_call" | custom-call | tf_op jit(solution)/shard_map/pack/pallas_call | solution.py:46
  1.9 0.0 copy-start.2
  2.0 33.1 %all-gather.4 = s16[128,128,128]{2,1,0:T(8,128)(2,1)S(1)} all-gather(s16[4,128,128]{2,1,0:T(8,128)(2,1)} %pack.1), channel_id=2, replica_groups=mesh['row'=32,'col'=16] {'row'}, dimensions={0}, use_global_device_ids=true | all-gather | bytes 4325376 | tf_op jit(solution)/shard_map/all_gather | solution.py:165
  35.1 0.0 copy-done.2
  35.1 41.3 %all-gather.5 = s16[64,128,128]{2,1,0:T(8,128)(2,1)S(1)} all-gather(s16[4,128,128]{2,1,0:T(8,128)(2,1)S(1)} %copy-done.2), channel_id=3, replica_groups=mesh['row'=32,'col'=16] {'col'}, dimensions={0}, use_global_device_ids=true | all-gather | bytes 2228224 | tf_op jit(solution)/shard_map/all_gather | solution.py:167
  76.4 0.0 copy-done.1
  76.4 0.0 copy-done
  76.4 6.2 %product.1 = s16[32,16,384]{2,1,0:T(8,128)(2,1)S(1)} custom-call(s32[64,64]{1,0:T(8,128)S(1)} %copy-done.1, s16[16,4,128,128]{3,2,1,0:T(8,128)(2,1)S(1)} %bitcast.3, s16[32,4,128,128]{3,2,1,0:T(8,128)(2,1)S(1)} %bitcast.2, s32[256,512]{1,0:T(8,128)S(1)} %copy-done), custom_call_target="tpu_custom_call" | custom-call | tf_op jit(solution)/shard_map/product/pallas_call | solution.py:120
  82.6 21.2 %all_to_all.5.x_ref = s16[32,16,384]{2,1,0:T(8,128)(2,1)S(1)} all-to-all(s16[32,16,384]{2,1,0:T(8,128)(2,1)S(1)} %product.1), channel_id=1, replica_groups=mesh['row'=32,'col'=16] {'row'}, dimensions={0} | all-to-all | bytes 786432 | tf_op jit(solution)/shard_map/all_to_all | solution.py:169
  103.8 1.0 scale.1
Async XLA Ops:
  0.0 76.4 %copy-start.1 = (s32[64,64]{1,0:T(8,128)S(1)}, s32[64,64]{1,0:T(8,128)}, u32[]{:S(2)}) copy-start(s32[64,64]{1,0:T(8,128)} %refs_0_.1) | copy-start | bytes 49156
  0.0 76.4 %copy-start = (s32[256,512]{1,0:T(8,128)S(1)}, s32[256,512]{1,0:T(8,128)}, u32[]{:S(2)}) copy-start(s32[256,512]{1,0:T(8,128)} %refs_3_.1) | copy-start | bytes 1572868
  1.9 33.1 %copy-start.2 = (s16[4,128,128]{2,1,0:T(8,128)(2,1)S(1)}, s16[4,128,128]{2,1,0:T(8,128)(2,1)}, u32[]{:S(2)}) copy-start(s16[4,128,128]{2,1,0:T(8,128)(2,1)} %pack.1) | copy-start | bytes 393220

commit v10 on v8

--- a/solution.py
+++ b/solution.py
@@ -72,26 +72,34 @@
     return tasks
 
 
-def product_body(rows, cols, live_hbm, a_ref, b_ref, keep_ref, out_ref, live, a_dense, b_dense, total, arrived):
-    flags_in = pltpu.make_async_copy(live_hbm, live, arrived)
-    flags_in.start()
+def product_body(rows, cols, live_hbm, a_ref, b_ref, keep_ref, out_ref, live, own, a_dense, b_dense, total, arrived):
     panels = a_ref.shape[0]
     each = b_ref.shape[0] // panels
     top, left = lax.axis_index("row") * rows, lax.axis_index("col") * cols
+    group = pl.multiple_of(top // GROUP * GROUP, GROUP)
+    behind = live.shape[0] - GROUP
+    first = pltpu.make_async_copy(live_hbm.at[pl.ds(0, GROUP)], live.at[pl.ds(0, GROUP)], arrived.at[0])
+    mine = pltpu.make_async_copy(live_hbm.at[pl.ds(group, GROUP)], own, arrived.at[1])
+    rest = pltpu.make_async_copy(live_hbm.at[pl.ds(GROUP, behind)], live.at[pl.ds(GROUP, behind)], arrived.at[2])
+    for flags in (first, mine, rest):
+        flags.start()
 
     def tasks_of(panel):
         a_to, b_to = a_dense.at[panel % 2], b_dense.at[panel % 2]
-        tasks = placing(live, top, panel * cols, rows, cols, a_ref.at[panel], a_to, 0, 0)
+        tasks = placing(own, top - group, panel * cols, rows, cols, a_ref.at[panel], a_to, 0, 0)
         for e in range(each):
-            group = panel * each + e
-            tasks += placing(live, group * rows, left, rows, cols, b_ref.at[group], b_to, 0, e * rows * TILE)
+            block = panel * each + e
+            tasks += placing(live, block * rows, left, rows, cols, b_ref.at[block], b_to, 0, e * rows * TILE)
         return tasks
 
     keep = keep_ref[...].astype(jnp.float32).T * (1.0 / (UNIT * UNIT))
-    flags_in.wait()
+    first.wait()
+    mine.wait()
     for place in tasks_of(0):
         place()
     for panel in range(panels):
+        if panel + 1 == GROUP // (each * rows):
+            rest.wait()
         later = tasks_of(panel + 1) if panel + 1 < panels else []
         share, high = len(later) // PARTS, total.shape[0] // PARTS
         for part in range(PARTS):
@@ -124,10 +132,11 @@
         out_specs=in_vmem,
         scratch_shapes=[
             pltpu.SMEM(tile_live.shape, tile_live.dtype),
+            pltpu.SMEM((GROUP, tile_live.shape[1]), tile_live.dtype),
             pltpu.VMEM((2, width, height), jnp.bfloat16),
             pltpu.VMEM((2, width, width), jnp.bfloat16),
             pltpu.VMEM((width, height), jnp.float32),
-            pltpu.SemaphoreType.DMA,
+            pltpu.SemaphoreType.DMA((3,)),
         ],
         compiler_params=pltpu.CompilerParams(vmem_limit_bytes=32 * 1024 * 1024),
         name="product",

time: 104 us -> 104 us (level)
    all_gather x1, blocking collectives: 34.9 us -> 36.1 us  [shards(): col_panel = lax.all_gather(packed, 'row', axis=0)]
where the time goes in v10:
time: 104 us
  blocking collectives  95 us (91%)
  Pallas kernels  8.69 us (8%)
    all_gather x1, blocking collectives, shards(): row_panel = lax.all_gather(packed, 'col', axis=0)  43.9 us
    all_gather x1, blocking collectives, shards(): col_panel = lax.all_gather(packed, 'row', axis=0)  36.1 us
    all_to_all x1, blocking collectives, shards(): lax.all_to_all(strips, 'row', split_axis=0, concat_axis=0, tiled=True)  15 us
    pallas_call x1, Pallas kernels, product(): pl.pallas_call(lambda *refs: product_body(rows, cols, *refs), out_shape=j...  5.71 us

profile of v10, /device:TPU:1, one launch (start us, length us, event | category | flops | bytes accessed | tf_op | source)
XLA Modules:
  0.0 103.7 jit_solution(18226390916472730670)
XLA Ops:
  0.0 0.0 copy-start.1
  0.0 0.0 copy-start
  0.0 1.9 %pack.1 = s16[4,128,128]{2,1,0:T(8,128)(2,1)} custom-call(s32[64,64]{1,0:T(8,128)} %refs_0_.1, bf16[256,512]{1,0:T(8,128)(2,1)} %x_hbm.1), custom_call_target="tpu_custom_call" | custom-call | tf_op jit(solution)/shard_map/pack/pallas_call | solution.py:46
  1.9 43.9 %all-gather.4 = s16[64,128,128]{2,1,0:T(8,128)(2,1)S(1)} all-gather(s16[4,128,128]{2,1,0:T(8,128)(2,1)} %pack.1), channel_id=2, replica_groups=mesh['row'=32,'col'=16] {'col'}, dimensions={0}, use_global_device_ids=true | all-gather | bytes 2228224 | tf_op jit(solution)/shard_map/all_gather | solution.py:174
  45.9 36.1 %all-gather.5 = s16[128,128,128]{2,1,0:T(8,128)(2,1)S(1)} all-gather(s16[4,128,128]{2,1,0:T(8,128)(2,1)} %pack.1), channel_id=3, replica_groups=mesh['row'=32,'col'=16] {'row'}, dimensions={0}, use_global_device_ids=true | all-gather | bytes 4325376 | tf_op jit(solution)/shard_map/all_gather | solution.py:175
  82.0 0.0 copy-done.1
  82.0 0.0 copy-done
  82.0 5.7 %product.1 = s16[32,16,384]{2,1,0:T(8,128)(2,1)S(1)} custom-call(s32[64,64]{1,0:T(8,128)S(1)} %copy-done.1, s16[16,4,128,128]{3,2,1,0:T(8,128)(2,1)S(1)} %bitcast.3, s16[32,4,128,128]{3,2,1,0:T(8,128)(2,1)S(1)} %bitcast.2, s32[256,512]{1,0:T(8,128)S(1)} %copy-done), custom_call_target="tpu_custom_call" | custom-call | tf_op jit(solution)/shard_map/product/pallas_call | solution.py:128
  87.7 15.0 %all_to_all.5.x_ref = s16[32,16,384]{2,1,0:T(8,128)(2,1)S(1)} all-to-all(s16[32,16,384]{2,1,0:T(8,128)(2,1)S(1)} %product.1), channel_id=1, replica_groups=mesh['row'=32,'col'=16] {'row'}, dimensions={0} | all-to-all | bytes 786432 | tf_op jit(solution)/shard_map/all_to_all | solution.py:177
  102.7 1.0 %scale.1 = f32[1,16,8192]{2,1,0:T(8,128)} custom-call(s16[32,16,384]{2,1,0:T(8,128)(2,1)S(1)} %all_to_all.5.x_ref), custom_call_target="tpu_custom_call" | custom-call | tf_op jit(solution)/shard_map/scale/pallas_call | solution.py:162
Async XLA Ops:
  0.0 82.0 %copy-start.1 = (s32[64,64]{1,0:T(8,128)S(1)}, s32[64,64]{1,0:T(8,128)}, u32[]{:S(2)}) copy-start(s32[64,64]{1,0:T(8,128)} %refs_0_.1) | copy-start | bytes 49156
  0.0 82.0 %copy-start = (s32[256,512]{1,0:T(8,128)S(1)}, s32[256,512]{1,0:T(8,128)}, u32[]{:S(2)}) copy-start(s32[256,512]{1,0:T(8,128)} %refs_3_.1) | copy-start | bytes 1572868

commit v11 on v10

--- a/solution.py
+++ b/solution.py
@@ -13,6 +13,7 @@
 SMALLEST = 2.0**-20
 PARTS = 2
 GROUP = 8
+CHUNKS = 4
 
 
 def spots(rows, cols):
@@ -24,15 +25,18 @@
     top, left = lax.axis_index("row") * rows, lax.axis_index("col") * cols
     group = pl.multiple_of(top // GROUP * GROUP, GROUP)
     flags_in = pltpu.make_async_copy(live_hbm.at[pl.ds(group, GROUP)], live, arrived.at[0])
-    block_in = pltpu.make_async_copy(x_hbm, x_ref, arrived.at[1])
+    lines = [pl.ds(a * TILE, TILE) for a in range(rows)]
+    block_in = [pltpu.make_async_copy(x_hbm.at[at], x_ref.at[at], arrived.at[1 + a]) for a, at in enumerate(lines)]
     flags_in.start()
-    block_in.start()
+    for line in block_in:
+        line.start()
     flags_in.wait()
-    block_in.wait()
     top = top - group
     slot = jnp.int32(0)
     for a, b, across, down in spots(rows, cols):
         flag = live[top + a, left + b]
+        if b == 0:
+            block_in[a].wait()
 
         @pl.when((flag > 0) & (slot < LIVE))
         def _(slot=slot, across=across, down=down):
@@ -51,7 +55,7 @@
         scratch_shapes=[
             pltpu.SMEM((GROUP, tile_live.shape[1]), tile_live.dtype),
             pltpu.VMEM(transition.shape, transition.dtype),
-            pltpu.SemaphoreType.DMA((2,)),
+            pltpu.SemaphoreType.DMA((1 + transition.shape[0] // TILE,)),
         ],
         name="pack",
     )(tile_live, transition)
@@ -143,7 +147,7 @@
     )(tile_live, row_panel, col_panel, keep)
 
 
-def scale_body(x_ref, out_ref):
+def scale_body(x_ref, out_hbm, out_ref, sent):
     parts, strips, height = x_ref.shape
     height = height - TILE
     nodes = parts * height
@@ -152,8 +156,16 @@
     entries = jnp.concatenate([part * part for part in kept], axis=2)
     column_total = jnp.sum(jnp.sum(entries, axis=0), axis=1, keepdims=True)
     factor = nodes / column_total
+    copies = []
     for p in range(parts):
-        out_ref[0, :, p * height : (p + 1) * height] = entries[p] * factor
+        out_ref[:, p * height : (p + 1) * height] = entries[p] * factor
+        if (p + 1) % (parts // CHUNKS) == 0:
+            chunk = p * CHUNKS // parts
+            span = slice(chunk * nodes // CHUNKS, (chunk + 1) * nodes // CHUNKS)
+            copies.append(pltpu.make_async_copy(out_ref.at[:, span], out_hbm.at[0, :, span], sent.at[chunk]))
+            copies[-1].start()
+    for copy in copies:
+        copy.wait()
 
 
 def scale(entries):
@@ -163,7 +175,8 @@
         scale_body,
         out_shape=jax.ShapeDtypeStruct((1, strips, parts * height), jnp.float32),
         in_specs=[pl.BlockSpec(memory_space=pltpu.VMEM)],
-        out_specs=pl.BlockSpec(memory_space=pltpu.VMEM),
+        out_specs=pl.BlockSpec(memory_space=pl.ANY),
+        scratch_shapes=[pltpu.VMEM((strips, parts * height), jnp.float32), pltpu.SemaphoreType.DMA((CHUNKS,))],
         compiler_params=pltpu.CompilerParams(vmem_limit_bytes=4 * 1024 * 1024),
         name="scale",
     )(entries)

time: 104 us -> 104 us (level)
  no operation moved by 1% of the time
where the time goes in v11:
time: 104 us
  blocking collectives  95 us (91%)
  Pallas kernels  8.66 us (8%)
    all_gather x1, blocking collectives, shards(): row_panel = lax.all_gather(packed, 'col', axis=0)  44.7 us
    all_gather x1, blocking collectives, shards(): col_panel = lax.all_gather(packed, 'row', axis=0)  35.1 us
    all_to_all x1, blocking collectives, shards(): lax.all_to_all(strips, 'row', split_axis=0, concat_axis=0, tiled=True)  15.3 us
    pallas_call x1, Pallas kernels, product(): pl.pallas_call(lambda *refs: product_body(rows, cols, *refs), out_shape=j...  5.71 us

profile of v11, /device:TPU:1, one launch (start us, length us, event | category | flops | bytes accessed | tf_op | source)
XLA Modules:
  0.0 103.7 jit_solution(12064901938422465648)
XLA Ops:
  0.0 0.0 copy-start.1
  0.0 0.0 copy-start
  0.0 1.9 %pack.1 = s16[4,128,128]{2,1,0:T(8,128)(2,1)} custom-call(s32[64,64]{1,0:T(8,128)} %refs_0_.1, bf16[256,512]{1,0:T(8,128)(2,1)} %x_hbm.1), custom_call_target="tpu_custom_call" | custom-call | tf_op jit(solution)/shard_map/pack/pallas_call | solution.py:50
  1.9 44.7 %all-gather.4 = s16[64,128,128]{2,1,0:T(8,128)(2,1)S(1)} all-gather(s16[4,128,128]{2,1,0:T(8,128)(2,1)} %pack.1), channel_id=2, replica_groups=mesh['row'=32,'col'=16] {'col'}, dimensions={0}, use_global_device_ids=true | all-gather | bytes 2228224 | tf_op jit(solution)/shard_map/all_gather | solution.py:187
  46.6 35.1 %all-gather.5 = s16[128,128,128]{2,1,0:T(8,128)(2,1)S(1)} all-gather(s16[4,128,128]{2,1,0:T(8,128)(2,1)} %pack.1), channel_id=3, replica_groups=mesh['row'=32,'col'=16] {'row'}, dimensions={0}, use_global_device_ids=true | all-gather | bytes 4325376 | tf_op jit(solution)/shard_map/all_gather | solution.py:188
  81.7 0.0 copy-done.1
  81.7 0.0 copy-done
  81.7 5.7 %product.1 = s16[32,16,384]{2,1,0:T(8,128)(2,1)S(1)} custom-call(s32[64,64]{1,0:T(8,128)S(1)} %copy-done.1, s16[16,4,128,128]{3,2,1,0:T(8,128)(2,1)S(1)} %bitcast.3, s16[32,4,128,128]{3,2,1,0:T(8,128)(2,1)S(1)} %bitcast.2, s32[256,512]{1,0:T(8,128)S(1)} %copy-done), custom_call_target="tpu_custom_call" | custom-call | tf_op jit(solution)/shard_map/product/pallas_call | solution.py:132
  87.4 15.3 %all_to_all.5.x_ref = s16[32,16,384]{2,1,0:T(8,128)(2,1)S(1)} all-to-all(s16[32,16,384]{2,1,0:T(8,128)(2,1)S(1)} %product.1), channel_id=1, replica_groups=mesh['row'=32,'col'=16] {'row'}, dimensions={0} | all-to-all | bytes 786432 | tf_op jit(solution)/shard_map/all_to_all | solution.py:190
  102.7 1.1 %scale.1 = f32[1,16,8192]{2,1,0:T(8,128)} custom-call(s16[32,16,384]{2,1,0:T(8,128)(2,1)S(1)} %all_to_all.5.x_ref), custom_call_target="tpu_custom_call" | custom-call | tf_op jit(solution)/shard_map/scale/pallas_call | solution.py:174
Async XLA Ops:
  0.0 81.7 %copy-start.1 = (s32[64,64]{1,0:T(8,128)S(1)}, s32[64,64]{1,0:T(8,128)}, u32[]{:S(2)}) copy-start(s32[64,64]{1,0:T(8,128)} %refs_0_.1) | copy-start | bytes 49156
  0.0 81.7 %copy-start = (s32[256,512]{1,0:T(8,128)S(1)}, s32[256,512]{1,0:T(8,128)}, u32[]{:S(2)}) copy-start(s32[256,512]{1,0:T(8,128)} %refs_3_.1) | copy-start | bytes 1572868

commit v12 on v11

--- a/solution.py
+++ b/solution.py
@@ -12,6 +12,7 @@
 OCTAVE = 0.6931471805599453 / 1024
 SMALLEST = 2.0**-20
 PARTS = 2
+PAIR = 2
 GROUP = 8
 CHUNKS = 4
 
@@ -88,12 +89,16 @@
     for flags in (first, mine, rest):
         flags.start()
 
-    def tasks_of(panel):
-        a_to, b_to = a_dense.at[panel % 2], b_dense.at[panel % 2]
-        tasks = placing(own, top - group, panel * cols, rows, cols, a_ref.at[panel], a_to, 0, 0)
-        for e in range(each):
-            block = panel * each + e
-            tasks += placing(live, block * rows, left, rows, cols, b_ref.at[block], b_to, 0, e * rows * TILE)
+    def tasks_of(pair):
+        a_to, b_to = a_dense.at[pair % 2], b_dense.at[pair % 2]
+        tasks = []
+        for p in range(PAIR):
+            panel = pair * PAIR + p
+            tasks += placing(own, top - group, panel * cols, rows, cols, a_ref.at[panel], a_to, p * cols * TILE, 0)
+            for e in range(each):
+                block = panel * each + e
+                across = (p * each + e) * rows * TILE
+                tasks += placing(live, block * rows, left, rows, cols, b_ref.at[block], b_to, 0, across)
         return tasks
 
     keep = keep_ref[...].astype(jnp.float32).T * (1.0 / (UNIT * UNIT))
@@ -101,10 +106,10 @@
     mine.wait()
     for place in tasks_of(0):
         place()
-    for panel in range(panels):
-        if panel + 1 == GROUP // (each * rows):
+    for panel in range(panels // PAIR):
+        if (panel + 1) * PAIR == GROUP // (each * rows):
             rest.wait()
-        later = tasks_of(panel + 1) if panel + 1 < panels else []
+        later = tasks_of(panel + 1) if (panel + 1) * PAIR < panels else []
         share, high = len(later) // PARTS, total.shape[0] // PARTS
         for part in range(PARTS):
             lines = slice(part * high, (part + 1) * high)
@@ -137,8 +142,8 @@
         scratch_shapes=[
             pltpu.SMEM(tile_live.shape, tile_live.dtype),
             pltpu.SMEM((GROUP, tile_live.shape[1]), tile_live.dtype),
-            pltpu.VMEM((2, width, height), jnp.bfloat16),
-            pltpu.VMEM((2, width, width), jnp.bfloat16),
+            pltpu.VMEM((2, PAIR * width, height), jnp.bfloat16),
+            pltpu.VMEM((2, width, PAIR * width), jnp.bfloat16),
             pltpu.VMEM((width, height), jnp.float32),
             pltpu.SemaphoreType.DMA((3,)),
         ],

time: 104 us -> 104 us (level)
    all_gather x1, blocking collectives: 35.1 us -> 36.3 us  [shards(): col_panel = lax.all_gather(packed, 'row', axis=0)]
where the time goes in v12:
time: 104 us
  blocking collectives  95.2 us (92%)
  Pallas kernels  9.19 us (9%)
    all_gather x1, blocking collectives, shards(): row_panel = lax.all_gather(packed, 'col', axis=0)  43.7 us
    all_gather x1, blocking collectives, shards(): col_panel = lax.all_gather(packed, 'row', axis=0)  36.3 us
    all_to_all x1, blocking collectives, shards(): lax.all_to_all(strips, 'row', split_axis=0, concat_axis=0, tiled=True)  15.2 us
    pallas_call x1, Pallas kernels, product(): pl.pallas_call(lambda *refs: product_body(rows, cols, *refs), out_shape=j...  6.12 us

profile of v12, /device:TPU:1, one launch (start us, length us, event | category | flops | bytes accessed | tf_op | source)
XLA Modules:
  0.0 104.4 jit_solution(3318574942612108983)
XLA Ops:
  0.0 0.0 copy-start.1
  0.0 0.0 copy-start
  0.0 2.0 %pack.1 = s16[4,128,128]{2,1,0:T(8,128)(2,1)} custom-call(s32[64,64]{1,0:T(8,128)} %refs_0_.1, bf16[256,512]{1,0:T(8,128)(2,1)} %x_hbm.1), custom_call_target="tpu_custom_call" | custom-call | tf_op jit(solution)/shard_map/pack/pallas_call | solution.py:51
  2.0 43.7 %all-gather.4 = s16[64,128,128]{2,1,0:T(8,128)(2,1)S(1)} all-gather(s16[4,128,128]{2,1,0:T(8,128)(2,1)} %pack.1), channel_id=2, replica_groups=mesh['row'=32,'col'=16] {'col'}, dimensions={0}, use_global_device_ids=true | all-gather | bytes 2228224 | tf_op jit(solution)/shard_map/all_gather | solution.py:192
  45.8 36.3 %all-gather.5 = s16[128,128,128]{2,1,0:T(8,128)(2,1)S(1)} all-gather(s16[4,128,128]{2,1,0:T(8,128)(2,1)} %pack.1), channel_id=3, replica_groups=mesh['row'=32,'col'=16] {'row'}, dimensions={0}, use_global_device_ids=true | all-gather | bytes 4325376 | tf_op jit(solution)/shard_map/all_gather | solution.py:193
  82.0 0.0 copy-done.1
  82.0 0.0 copy-done
  82.0 6.1 %product.1 = s16[32,16,384]{2,1,0:T(8,128)(2,1)S(1)} custom-call(s32[64,64]{1,0:T(8,128)S(1)} %copy-done.1, s16[16,4,128,128]{3,2,1,0:T(8,128)(2,1)S(1)} %bitcast.3, s16[32,4,128,128]{3,2,1,0:T(8,128)(2,1)S(1)} %bitcast.2, s32[256,512]{1,0:T(8,128)S(1)} %copy-done), custom_call_target="tpu_custom_call" | custom-call | tf_op jit(solution)/shard_map/product/pallas_call | solution.py:137
  88.2 15.2 %all_to_all.5.x_ref = s16[32,16,384]{2,1,0:T(8,128)(2,1)S(1)} all-to-all(s16[32,16,384]{2,1,0:T(8,128)(2,1)S(1)} %product.1), channel_id=1, replica_groups=mesh['row'=32,'col'=16] {'row'}, dimensions={0} | all-to-all | bytes 786432 | tf_op jit(solution)/shard_map/all_to_all | solution.py:195
  103.3 1.1 %scale.1 = f32[1,16,8192]{2,1,0:T(8,128)} custom-call(s16[32,16,384]{2,1,0:T(8,128)(2,1)S(1)} %all_to_all.5.x_ref), custom_call_target="tpu_custom_call" | custom-call | tf_op jit(solution)/shard_map/scale/pallas_call | solution.py:179
Async XLA Ops:
  0.0 82.0 %copy-start.1 = (s32[64,64]{1,0:T(8,128)S(1)}, s32[64,64]{1,0:T(8,128)}, u32[]{:S(2)}) copy-start(s32[64,64]{1,0:T(8,128)} %refs_0_.1) | copy-start | bytes 49156
  0.0 82.0 %copy-start = (s32[256,512]{1,0:T(8,128)S(1)}, s32[256,512]{1,0:T(8,128)}, u32[]{:S(2)}) copy-start(s32[256,512]{1,0:T(8,128)} %refs_3_.1) | copy-start | bytes 1572868
